TPU v7x, 768 devices: a whole 4x8x12 slice. The times are simulated.
768 devices in a mesh: slab: 64 (over z_hi, y, core), grp: 12 (over x, z_lo).
Axes of the slice: x: 4, y: 8, z: 12 (z_hi: 4, z_lo: 3; z = z_hi * 3 + z_lo), core: 2. Of those that a mesh axis runs over, the one named last changes fastest.
Arguments:
- initial_samples: bfloat16 [48, 128, 4, 12288], P('grp', 'slab'), may hold values from -6 to 6
- courant_east: float32 [128, 2, 12288], P('slab'), may hold values from -0.45 to 0.45
- northward_courant: float32 [128, 2, 12288], P('slab'), may hold values from -0.45 to 0.45
- diffusivity: float32 [8, 4], replicated, may hold values from 0.02 to 0.2
- profile_index: int32 [128], P('slab'), may hold values from 0 to 7
- observations: float32 [128, 4, 12288], P(None, None, ('slab', 'grp')), may hold values from -6 to 6
- error_precision: float32 [4], replicated, may hold values from 0.3 to 3
- localization: float32 [4, 256], replicated, may hold values from 0.05 to 1
- patch_tiles: int32 [8, 768], P(None, ('slab', 'grp')), may hold values from 0 to 3
- patch_counts: int32 [8, 768], P(None, ('slab', 'grp')), may hold values from 16 to 256, as said below
Outputs:
- analysis_state: bfloat16 [48, 128, 4, 12288], P('grp', 'slab')
Inputs may be any that keep to these rules, and one draw needn't show every extreme that they name: A patch observes its first patch_counts columns in row-major order; some patch observes all 256 columns and some exactly 16.
All inputs are finite; a program needn't handle non-finite values.
Results may differ from a plain program's by a relative error of at most 0.0052.
Values may be sent and summed in bfloat16 or wider, within the bound.
A program may use at most 64 MiB of HBM per device.

v0:
```python
import math

import jax
import jax.numpy as jnp
from jax import lax
from jax.sharding import PartitionSpec as P

PATCH = 16
NS_ITERS = 4


def with_halo(block, sides, width):
    for axis, dim in sides:
        count = lax.axis_size(axis)
        forward = [(i, i + 1) for i in range(count - 1)]
        backward = [(target, source) for source, target in forward]
        low = lax.ppermute(
            lax.slice_in_dim(block, block.shape[dim] - width, None, axis=dim), axis, forward
        )
        high = lax.ppermute(lax.slice_in_dim(block, 0, width, axis=dim), axis, backward)
        block = jnp.concatenate([low, block, high], axis=dim)
    return block


def advance_with(current, eastern, western, northern, southern, cour_east, cour_north, kappa):
    return (
        current
        - 0.5 * cour_east * (eastern - western)
        - 0.5 * cour_north * (northern - southern)
        + kappa * (eastern + western + northern + southern - 4.0 * current)
    )


def to_blocks(field, slab_count, group_count):
    lead, lat_rows, var_count, longitude_cells = field.shape
    lon_local = longitude_cells // (slab_count * group_count)
    parts = field.reshape(lead, lat_rows, var_count, slab_count, group_count, lon_local)
    parts = jnp.transpose(parts, (0, 3, 4, 1, 2, 5))
    return parts.reshape(lead, slab_count, group_count, lat_rows * var_count * lon_local)


def to_patches(field):
    lead, lat_cells, var_count, lon_local = field.shape
    row_count = lat_cells // PATCH
    col_count = lon_local // PATCH
    parts = field.reshape(lead, row_count, PATCH, var_count, col_count, PATCH)
    parts = jnp.transpose(parts, (0, 1, 4, 3, 2, 5))
    return parts.reshape(lead, row_count, col_count, var_count, PATCH * PATCH)


def from_patches(patches, lat_cells, lon_local):
    lead, row_count, col_count, var_count, cells = patches.shape
    parts = patches.reshape(lead, row_count, col_count, var_count, PATCH, PATCH)
    parts = jnp.transpose(parts, (0, 1, 4, 3, 2, 5))
    return parts.reshape(lead, lat_cells, var_count, lon_local)


def analyse_patches(
    ensemble, observed_values, error_precision, localization, patch_tiles, patch_counts, sweeps
):
    members = ensemble.shape[0]
    cells = ensemble.shape[-1]
    highest = lax.Precision.HIGHEST
    states = ensemble.astype(jnp.float32)
    average = jnp.mean(states, axis=0)
    deviation = states - average
    position = jnp.arange(cells, dtype=jnp.int32)
    observed = (position[None, None, :] < patch_counts[:, :, None]).astype(jnp.float32)
    tile_hot = (
        patch_tiles[:, :, None] == jnp.arange(localization.shape[0], dtype=jnp.int32)[None, None, :]
    ).astype(jnp.float32)
    weights = jnp.einsum("rct,tq->rcq", tile_hot, localization, precision=highest) * observed
    precision_map = weights[:, :, None, :] * error_precision[None, None, :, None]
    weighted = deviation * precision_map
    gram_matrix = jnp.einsum("krcvq,jrcvq->rckj", weighted, deviation, precision=highest)
    observation_misfit = observed_values - average
    driving = jnp.einsum("krcvq,rcvq->rck", weighted, observation_misfit, precision=highest)
    identity = jnp.eye(members, dtype=jnp.float32)
    system = (members - 1.0) * identity + gram_matrix
    trace_sum = jnp.trace(system, axis1=2, axis2=3)
    scaled_iter = system / trace_sum[:, :, None, None]
    root_iter = jnp.broadcast_to(identity, system.shape)
    for sweep in range(sweeps):
        correction = 1.5 * identity - 0.5 * jnp.matmul(root_iter, scaled_iter, precision=highest)
        scaled_iter = jnp.matmul(scaled_iter, correction, precision=highest)
        root_iter = jnp.matmul(correction, root_iter, precision=highest)
    root_inverse = root_iter / jnp.sqrt(trace_sum)[:, :, None, None]
    mean_weights = jnp.matmul(
        root_inverse,
        jnp.matmul(root_inverse, driving[..., None], precision=highest),
        precision=highest,
    )
    weights_all = math.sqrt(members - 1.0) * root_inverse + mean_weights
    analysis_increment = jnp.einsum("jrcvq,rcjk->krcvq", deviation, weights_all, precision=highest)
    return (average + analysis_increment).astype(jnp.bfloat16)


def regroup_in(blocks):
    moved = lax.all_to_all(
        lax.all_to_all(blocks, "slab", split_axis=1, concat_axis=1, tiled=True),
        "grp",
        split_axis=2,
        concat_axis=0,
        tiled=True,
    )
    return moved


def on_device(
    initial_samples,
    courant_east,
    northward_courant,
    diffusivity,
    profile_index,
    observations,
    error_precision,
    localization,
    patch_tiles,
    patch_counts,
):
    member_count, lat_rows, var_count, longitude_cells = initial_samples.shape
    slab_count = lax.axis_size("slab")
    group_count = lax.axis_size("grp")
    lon_local = observations.shape[2]
    lat_cells = observations.shape[0]
    level_count = courant_east.shape[1]
    variable_count = var_count // level_count
    all_members = member_count * group_count
    highest = lax.Precision.HIGHEST
    cour_east = jnp.repeat(courant_east, variable_count, axis=1)[None]
    cour_north = jnp.repeat(northward_courant, variable_count, axis=1)[None]
    profile_hot = (
        profile_index[:, None] == jnp.arange(diffusivity.shape[0], dtype=jnp.int32)[None, :]
    ).astype(jnp.float32)
    kappa = jnp.dot(profile_hot, diffusivity, precision=highest)[None, :, :, None]
    current = initial_samples.astype(jnp.float32)
    for sweep in range(2):
        padded = with_halo(current, (("slab", 1),), 1)
        eastern = jnp.roll(current, -1, axis=3)
        western = jnp.roll(current, 1, axis=3)
        current = advance_with(
            current, eastern, western, padded[:, 2:], padded[:, :-2], cour_east, cour_north, kappa
        )
    blocks = to_blocks(current.astype(jnp.bfloat16), slab_count, group_count)
    ensemble = regroup_in(blocks).reshape(all_members, lat_cells, var_count, lon_local)
    ensemble_patches = to_patches(ensemble)
    observed_patches = to_patches(observations[None])[0]
    updated_estimate = analyse_patches(
        ensemble_patches,
        observed_patches,
        error_precision,
        localization,
        patch_tiles,
        patch_counts,
        NS_ITERS,
    )
    domain_portions = from_patches(updated_estimate, lat_cells, lon_local)
    domain_portions = domain_portions.reshape(
        all_members, slab_count, 1, lat_rows * var_count * lon_local
    )
    returned = lax.all_to_all(
        lax.all_to_all(domain_portions, "slab", split_axis=1, concat_axis=1, tiled=True),
        "grp",
        split_axis=0,
        concat_axis=2,
        tiled=True,
    )
    returned = returned.reshape(
        member_count, slab_count, group_count, lat_rows, var_count, lon_local
    )
    returned = jnp.transpose(returned, (0, 3, 4, 1, 2, 5))
    return returned.reshape(member_count, lat_rows, var_count, longitude_cells)


def solution(mesh):
    return jax.shard_map(
        on_device,
        mesh=mesh,
        in_specs=(
            P("grp", "slab", None, None),
            P("slab", None, None),
            P("slab", None, None),
            P(),
            P("slab"),
            P(None, None, ("slab", "grp")),
            P(),
            P(),
            P(None, ("slab", "grp")),
            P(None, ("slab", "grp")),
        ),
        out_specs=P("grp", "slab", None, None),
        check_vma=False,
    )
```

profile of v0, /device:TPU:57, one launch (start us, length us, event | category | flops | bytes accessed | tf_op | source)
XLA Modules:
  0.0 311.1 jit_solution(15044878610255037018)
XLA Ops:
  0.0 2.5 fusion.60
  2.5 2.6 collective-permute-start
  5.1 7.0 %collective-permute-start.1 = (f32[4,1,4,12288]{3,2,1,0:T(4,128)}, f32[4,1,4,12288]{3,2,1,0:T(4,128)}, u32[]{:S(2)}, u32[]{:S(2)}) collective-permute-start(f32[4,1,4,12288]{3,2,1,0:T(4,128)} %get-tuple-element.15), channel_id=1, source_target_pairs={{0,12},{12,24},{24,36},{36,48},{48,60},{60,72},{72,84},{84,96},{96... | collective-permute-start | bytes 2359304 | tf_op jit(solution)/shard_map/ppermute | solution.py:17
  18.2 18.7 %collective-permute-done = f32[4,1,4,12288]{3,2,1,0:T(4,128)} collective-permute-done((f32[4,1,4,12288]{3,2,1,0:T(4,128)}, f32[4,1,4,12288]{3,2,1,0:T(4,128)}, u32[]{:S(2)}, u32[]{:S(2)}) %collective-permute-start) | collective-permute-done | bytes 786464 | tf_op jit(solution)/shard_map/ppermute | solution.py:20
  36.8 5.1 %multiply_add_fusion = f32[4,2,4,12288]{3,2,1,0:T(4,128)S(1)} fusion(f32[4,2,4,12288]{3,2,1,0:T(4,128)} %convert_element_type.49, f32[4,1,4,12288]{3,2,1,0:T(4,128)} %collective-permute-done, f32[4,1,4,12288]{3,2,1,0:T(4,128)} %collective-permute-done.1, f32[4,2,4,12287]{3,2,1,0:T(4,128)} %get-tuple-element.12, f32[4,2,4,1]{3,2,1,0:T(4,128)S(1)} %get-tuple-element.14, ...), kind=kLoop, calls=%fused_computation.26 | loop fusion | flops 6684672 | bytes 8650784 | tf_op jit(solution)/shard_map/add | solution.py:27
  43.9 7.5 %collective-permute-start.3 = (f32[4,1,4,12288]{3,2,1,0:T(4,128)S(1)}, f32[4,1,4,12288]{3,2,1,0:T(4,128)S(1)}, u32[]{:S(2)}, u32[]{:S(2)}) collective-permute-start(f32[4,1,4,12288]{3,2,1,0:T(4,128)S(1)} %get-tuple-element.9), channel_id=1, source_target_pairs={{0,12},{12,24},{24,36},{36,48},{48,60},{60,72},{72,84},{84,96},{96... | collective-permute-start | bytes 2359304 | tf_op jit(solution)/shard_map/ppermute | solution.py:17
  52.5 22.7 %collective-permute-done.2 = f32[4,1,4,12288]{3,2,1,0:T(4,128)S(1)} collective-permute-done((f32[4,1,4,12288]{3,2,1,0:T(4,128)S(1)}, f32[4,1,4,12288]{3,2,1,0:T(4,128)S(1)}, u32[]{:S(2)}, u32[]{:S(2)}) %collective-permute-start.2) | collective-permute-done | bytes 786464 | tf_op jit(solution)/shard_map/ppermute | solution.py:20
  75.2 3.2 %add_convert_fusion = bf16[4,2,4,12288]{3,2,1,0:T(4,128)(2,1)S(1)} fusion(f32[4,2,4,12288]{3,2,1,0:T(4,128)S(1)} %multiply_add_fusion, f32[4,1,4,12288]{3,2,1,0:T(4,128)S(1)} %collective-permute-done.2, f32[4,1,4,12288]{3,2,1,0:T(4,128)S(1)} %collective-permute-done.3, f32[4,2,4,12287]{3,2,1,0:T(4,128)S(1)} %get-tuple-element.6, ...), kind=kLoop, calls=%fused_computation.25 | loop fusion | flops 7077888 | bytes 7864352 | tf_op jit(solution)/shard_map/convert_element_type | solution.py:144
  78.4 9.1 %reshape.184 = bf16[4,2,4,64,12,16]{5,4,3,2,1,0:T(8,128)(2,1)} reshape(bf16[4,2,4,12288]{3,2,1,0:T(4,128)(2,1)S(1)} %add_convert_fusion) | data formatting | bytes 1572864 | tf_op jit(solution)/shard_map/reshape | solution.py:37
  87.5 9.3 %copy.62 = bf16[4,64,12,2,4,16]{1,5,4,3,2,0:T(8,128)(2,1)S(1)} copy(bf16[4,64,12,2,4,16]{5,2,1,4,3,0:T(8,128)(2,1)} %bitcast.100) | data formatting | bytes 1572864 | tf_op jit(solution)/shard_map/transpose | solution.py:38
  97.6 48.5 %all_to_all.37 = bf16[4,64,12,128]{3,0,2,1:T(4,128)(2,1)S(1)} all-to-all(bf16[4,64,12,128]{3,0,2,1:T(4,128)(2,1)S(1)} %copy.63), channel_id=1, replica_groups=mesh['slab'=64,'grp'=12] {'slab'}, dimensions={1} | all-to-all | bytes 1572864 | tf_op jit(solution)/shard_map/all_to_all | solution.py:100
  147.3 5.1 %all-to-all-start.1 = ((bf16[4,64,12,128]{3,1,0,2:T(8,128)(2,1)}), bf16[4,64,12,128]{3,1,0,2:T(8,128)(2,1)S(1)}, u32[]{:S(2)}, u32[]{:S(2)}) async-start(bf16[4,64,12,128]{3,1,0,2:T(8,128)(2,1)} %copy.64), calls=%async_computation.1 | async-start | bytes 1572864 | tf_op jit(solution)/shard_map/all_to_all | solution.py:99
  153.1 14.1 %all-to-all-done.1 = bf16[4,64,12,128]{3,1,0,2:T(8,128)(2,1)S(1)} async-done(((bf16[4,64,12,128]{3,1,0,2:T(8,128)(2,1)}), bf16[4,64,12,128]{3,1,0,2:T(8,128)(2,1)S(1)}, u32[]{:S(2)}, u32[]{:S(2)}) %all-to-all-start.1) | async-done | bytes 786464 | tf_op jit(solution)/shard_map/all_to_all | solution.py:99
  167.9 9.9 %reshape.192 = f32[48,8,16,4,1,16]{5,3,2,1,0,4:T(4,128)} reshape(f32[12,4,64,1,128]{4,2,1,0,3:T(8,128)S(1)} %convert_bitcast_fusion) | data formatting | bytes 3145728 | tf_op jit(solution)/shard_map/convert_element_type | solution.py:64
  177.8 12.5 %copy.69 = f32[48,8,1,4,16,16]{0,5,4,3,1,2:T(8,128)} copy(f32[48,8,1,4,16,16]{5,3,4,1,0,2:T(4,128)} %bitcast.99) | data formatting | bytes 3145728 | tf_op jit(solution)/shard_map/convert_element_type | solution.py:64
  190.2 13.3 %select_reduce_fusion = (f32[8]{0:T(128)S(1)}, f32[8,48,48]{2,1,0:T(8,128)S(1)}) fusion(pred[48,48]{1,0:T(8,128)(4,1)S(1)} %iota_compare_fusion, f32[48,8,4,256]{0,3,2,1:T(8,128)} %bitcast.96, f32[8,4,256]{2,1,0:T(4,128)S(1)} %copy.68, f32[8,4,256]{2,1,0:T(4,128)S(1)} %broadcast_multiply_fusion.3, f32[48,48]{1,0:T(8,128)S(1)} %fusion.46), kind=kOutput, calls=%fused_computation.45 | convolution fusion | flops 227727360 | bytes 1723680 | tf_op jit(solution)/shard_map/krcvq,jrcvq->rckj/dot_general | solution.py:75
  206.6 4.3 %fusion.33 = f32[8,48,1]{1,2,0:T(1,128)S(1)} fusion(f32[48,8,4,256]{0,3,2,1:T(8,128)S(1)} %bitcast.97, f32[8,4,256]{2,1,0:T(4,128)S(1)} %broadcast_multiply_fusion.3, f32[8,4,256]{2,1,0:T(4,128)S(1)} %copy.68, f32[8,4,256,1]{2,0,1,3:T(8,128)S(1)} %subtract_bitcast_fusion), kind=kOutput, calls=%fused_computation.40 | convolution fusion | flops 5505024 | bytes 1672704 | tf_op jit(solution)/shard_map/krcvq,rcvq->rck/dot_general | solution.py:77
  212.4 6.1 %fusion.16 = bf16[48,8,1,4,256]{4,0,3,1,2:T(8,128)(2,1)S(1)} fusion(f32[48,8,4,256]{0,3,2,1:T(8,128)S(1)} %bitcast.98, f32[8,4,256]{2,1,0:T(4,128)S(1)} %copy.68, f32[8,48,48]{2,1,0:T(8,128)S(1)} %convolution_divide_fusion, f32[8,48]{1,0:T(8,128)S(1)} %bitcast.108), kind=kOutput, calls=%fused_computation.27 | convolution fusion | flops 227708928 | bytes 2467328 | tf_op jit(solution)/shard_map/jrcvq,rcjk->krcvq/dot_general | solution.py:94
  219.6 1.9 copy.77
  221.5 2.0 copy.78
  223.5 48.3 %all_to_all.38 = bf16[48,64,1,128]{3,0,2,1:T(8,128)(2,1)S(1)} all-to-all(bf16[48,64,1,128]{3,0,2,1:T(8,128)(2,1)S(1)} %copy.78), channel_id=1, replica_groups=mesh['slab'=64,'grp'=12] {'slab'}, dimensions={1} | all-to-all | bytes 1572864 | tf_op jit(solution)/shard_map/all_to_all | solution.py:162
  272.0 20.5 %all_to_all.39 = bf16[48,64,1,128]{3,1,2,0:T(8,128)(2,1)S(1)} all-to-all(bf16[48,64,1,128]{3,1,2,0:T(8,128)(2,1)S(1)} %copy.79), channel_id=1, replica_groups=mesh['slab'=64,'grp'=12] {'grp'}, dimensions={0} | all-to-all | bytes 1572864 | tf_op jit(solution)/shard_map/all_to_all | solution.py:161
  293.3 7.7 %copy.81 = bf16[4,2,4,64,12,16]{5,4,3,2,1,0:T(8,128)(2,1)} copy(bf16[4,2,4,64,12,16]{3,5,2,1,4,0:T(8,128)(2,1)S(1)} %bitcast.104) | data formatting | bytes 1572864 | tf_op jit(solution)/shard_map/transpose | solution.py:171
  301.0 10.1 %reshape.188 = bf16[4,2,4,12288]{3,2,1,0:T(4,128)(2,1)} reshape(bf16[4,2,4,64,12,16]{5,4,3,2,1,0:T(8,128)(2,1)} %copy.81) | data formatting | bytes 1572864 | tf_op jit(solution)/shard_map/reshape | solution.py:172
  (75 shorter events, 18.8 us)
Async XLA Ops:
  0.0 152.8 %copy-start = (f32[4,256]{1,0:T(4,128)S(1)}, f32[4,256]{1,0:T(4,128)}, u32[]{:S(2)}) copy-start(f32[4,256]{1,0:T(4,128)} %param.17) | copy-start | bytes 12292
  0.0 12.1 %copy-start.3 = (bf16[4,2,4,12288]{3,2,1,0:T(4,128)(2,1)S(1)}, bf16[4,2,4,12288]{3,2,1,0:T(4,128)(2,1)}, u32[]{:S(2)}) copy-start(bf16[4,2,4,12288]{3,2,1,0:T(4,128)(2,1)} %param.10) | copy-start | bytes 2359300
  2.5 34.4 %collective-permute-start = (f32[4,1,4,12288]{3,2,1,0:T(4,128)}, f32[4,1,4,12288]{3,2,1,0:T(4,128)}, u32[]{:S(2)}, u32[]{:S(2)}) collective-permute-start(f32[4,1,4,12288]{3,2,1,0:T(4,128)} %get-tuple-element.16), channel_id=1, source_target_pairs={{12,0},{24,12},{36,24},{48,36},{60,48},{72,60},{84,72},{96,84},{10... | collective-permute-start | bytes 2359304 | tf_op jit(solution)/shard_map/ppermute | solution.py:20
  5.0 8.8 %copy-start.4 = (f32[2,2,12288]{2,1,0:T(2,128)S(1)}, f32[2,2,12288]{2,1,0:T(2,128)}, u32[]{:S(2)}) copy-start(f32[2,2,12288]{2,1,0:T(2,128)} %param.11) | copy-start | bytes 589828
  5.1 8.9 %copy-start.5 = (f32[2,2,12288]{2,1,0:T(2,128)S(1)}, f32[2,2,12288]{2,1,0:T(2,128)}, u32[]{:S(2)}) copy-start(f32[2,2,12288]{2,1,0:T(2,128)} %param.12) | copy-start | bytes 589828
  5.1 31.8 %collective-permute-start.1 = (f32[4,1,4,12288]{3,2,1,0:T(4,128)}, f32[4,1,4,12288]{3,2,1,0:T(4,128)}, u32[]{:S(2)}, u32[]{:S(2)}) collective-permute-start(f32[4,1,4,12288]{3,2,1,0:T(4,128)} %get-tuple-element.15), channel_id=1, source_target_pairs={{0,12},{12,24},{24,36},{36,48},{48,60},{60,72},{72,84},{84,96},{96... | collective-permute-start | bytes 2359304 | tf_op jit(solution)/shard_map/ppermute | solution.py:17
  16.0 1.9 copy-start.8
  16.0 1.9 copy-start.9
  42.0 33.2 %collective-permute-start.2 = (f32[4,1,4,12288]{3,2,1,0:T(4,128)S(1)}, f32[4,1,4,12288]{3,2,1,0:T(4,128)S(1)}, u32[]{:S(2)}, u32[]{:S(2)}) collective-permute-start(f32[4,1,4,12288]{3,2,1,0:T(4,128)S(1)} %get-tuple-element.10), channel_id=1, source_target_pairs={{12,0},{24,12},{36,24},{48,36},{60,48},{72,60},{84,72},{96,84},{10... | collective-permute-start | bytes 2359304 | tf_op jit(solution)/shard_map/ppermute | solution.py:20
  43.9 31.3 %collective-permute-start.3 = (f32[4,1,4,12288]{3,2,1,0:T(4,128)S(1)}, f32[4,1,4,12288]{3,2,1,0:T(4,128)S(1)}, u32[]{:S(2)}, u32[]{:S(2)}) collective-permute-start(f32[4,1,4,12288]{3,2,1,0:T(4,128)S(1)} %get-tuple-element.9), channel_id=1, source_target_pairs={{0,12},{12,24},{24,36},{36,48},{48,60},{60,72},{72,84},{84,96},{96... | collective-permute-start | bytes 2359304 | tf_op jit(solution)/shard_map/ppermute | solution.py:17
  146.2 6.3 %copy-start.6 = (f32[128,4,16]{0,2,1:T(8,128)S(1)}, f32[128,4,16]{0,2,1:T(8,128)}, u32[]{:S(2)}) copy-start(f32[128,4,16]{0,2,1:T(8,128)} %param.15) | copy-start | bytes 98308
  146.2 6.6 %copy-start.10 = (s32[8,1]{0,1:T(1,128)S(1)}, s32[8,1]{0,1:T(1,128)}, u32[]{:S(2)}) copy-start(s32[8,1]{0,1:T(1,128)} %param.19) | copy-start | bytes 100
  146.2 6.6 %copy-start.11 = (s32[8,1]{0,1:T(1,128)S(1)}, s32[8,1]{0,1:T(1,128)}, u32[]{:S(2)}) copy-start(s32[8,1]{0,1:T(1,128)} %param.18) | copy-start | bytes 100
  147.3 5.7 %copy-start.7 = (f32[4]{0:T(128)S(1)}, f32[4]{0:T(128)}, u32[]{:S(2)}) copy-start(f32[4]{0:T(128)} %param.16) | copy-start | bytes 52
  147.3 19.9 %all-to-all-start.1 = ((bf16[4,64,12,128]{3,1,0,2:T(8,128)(2,1)}), bf16[4,64,12,128]{3,1,0,2:T(8,128)(2,1)S(1)}, u32[]{:S(2)}, u32[]{:S(2)}) async-start(bf16[4,64,12,128]{3,1,0,2:T(8,128)(2,1)} %copy.64), calls=%async_computation.1 | async-start | bytes 1572864 | tf_op jit(solution)/shard_map/all_to_all | solution.py:99
  203.9 2.7 copy-start.2
  301.0 10.1 %copy-start.1 = (f32[4,256]{1,0:T(4,128)S(1)}, f32[4,256]{1,0:T(4,128)}, u32[]{:S(2)}) copy-start(f32[4,256]{1,0:T(4,128)} %param.17) | copy-start | bytes 12292
where the time goes:
time: 315 us; the launch traced here: 311 us
  blocking collectives  117 us (37%)
  local copies, waits for them, and re-layouts  74.4 us (24%)
  waiting for transfers between devices  55.5 us (18%)
  matrix products  28.5 us (9%)
  starting transfers between devices  24.2 us (8%)
  other arithmetic  10.8 us (3%)
    all_to_all x1, blocking collectives, regroup_in(): lax.all_to_all(blocks, 'slab', split_axis=1, concat_axis=1, tiled=True)  48.5 us
    all_to_all x1, blocking collectives, on_device(): lax.all_to_all(domain_portions, 'slab', split_axis=1, concat_axis=1, tile...  48.3 us
    ppermute x2, waiting for transfers between devices, with_halo(): lax.ppermute(lax.slice_in_dim(block, 0, width, axis=dim), axis, backward)  41.4 us
    convert_element_type x2, local copies, waits for them, and re-layouts, analyse_patches(): states = ensemble.astype(jnp.float32)  22.3 us
    all_to_all x1, blocking collectives, on_device(): lax.all_to_all(lax.all_to_all(domain_portions, 'slab', split_axis=1, conc...  20.5 us
    ppermute x2, starting transfers between devices, with_halo(): lax.ppermute(lax.slice_in_dim(block, block.shape[dim] - width, None, axis...  14.6 us
    all_to_all x1, waiting for transfers between devices, regroup_in(): lax.all_to_all(lax.all_to_all(blocks, 'slab', split_axis=1, concat_axis=1...  14.1 us
    dot_general x1, matrix products, analyse_patches(): jnp.einsum('krcvq,jrcvq->rckj', weighted, deviation, precision=highest)  13.3 us
  transfers between devices with their start and end apart: 5, of which 3 were waited for; matrix products, arithmetic and copies ran while one was open for 2% of the time, Pallas kernels for 0%

commit v1 on v0

v1 whole, which is shorter than its diff:
```python
import functools
import math

import jax
import jax.numpy as jnp
from jax import lax
from jax.experimental import pallas as pl
from jax.experimental.pallas import tpu as pltpu
from jax.sharding import PartitionSpec as P

PATCH = 16
NS_ITERS = 4
F32 = jnp.float32
BF16 = jnp.bfloat16
VMEM_LIMIT = 56 * 1024 * 1024
LANES = 128
ROWS = 8
PAD = 64


def lane_ids(rows):
    return lax.broadcasted_iota(jnp.int32, (rows, LANES), 1)


def pack_kernel(groups, prof_ref, diff_ref, x_ref, ce_ref, cn_ref, s_ref, c_ref):
    blocks = ROWS * groups
    me = lax.axis_index("grp")
    lane4 = lane_ids(4)

    def tiles(b):
        at = pl.ds(pl.multiple_of(b * LANES, LANES), LANES)
        return [[x_ref[m, r, :, at].astype(F32) for r in range(2)] for m in range(4)]

    def turned(x, r, v):
        return jnp.concatenate([x[m][r][v : v + 1] for m in range(4)], axis=0)

    def one(b, carry):
        x = tiles(b)
        for r in range(2):
            for v in range(4):
                s_ref[b, r * 4 + v] = turned(x, r, v).astype(BF16)
        return carry

    lax.fori_loop(0, blocks, one, 0)

    def edges(b, carry):
        before = lax.rem(b + blocks - 1, blocks)
        after = lax.rem(b + 1, blocks)
        packed = jnp.zeros((4, LANES), F32)
        for k in range(8):
            mixed = jnp.where(lane4 < 64, s_ref[after, k].astype(F32), s_ref[before, k].astype(F32))
            moved = pltpu.roll(mixed, 2 + 8 * k, 1)
            packed = jnp.where((lane4 >= 8 * k) & (lane4 < 8 * k + 4), moved, packed)
        s_ref[b, 8] = packed.astype(BF16)
        return carry

    lax.fori_loop(0, blocks, edges, 0)

    kappas = []
    for r in range(2):
        for v in range(4):
            kappas.append(jnp.full((1, LANES), diff_ref[prof_ref[r], v], F32))
    kappa = jnp.concatenate(kappas, axis=0)
    lane1 = lane_ids(1)
    kappa_lanes = jnp.zeros((1, LANES), F32)
    for k in range(8):
        kappa_lanes = jnp.where(lane1 // 8 == k, kappas[k], kappa_lanes)

    lane8 = lane_ids(8)
    sub8 = lax.broadcasted_iota(jnp.int32, (8, LANES), 0)
    mine = (lax.rem(sub8, 4) == lane8 // 16) & (lane8 < 64)

    def courant(b):
        at = pl.ds(pl.multiple_of(b * LANES, LANES), LANES)
        return jnp.concatenate([ce_ref[0, :, at], ce_ref[1, :, at], cn_ref[0, :, at], cn_ref[1, :, at]], axis=0)

    for i in range(ROWS):
        b = me * ROWS + i
        here = courant(b)
        before = courant(lax.rem(b + blocks - 1, blocks))
        after = courant(lax.rem(b + 1, blocks))
        low = jnp.broadcast_to(before[:, LANES - 1 : LANES], (8, LANES))
        high = jnp.broadcast_to(after[:, 0:1], (8, LANES))
        side = jnp.where(mine, jnp.where(lax.rem(lane8, 8) == 1, low, high), 0.0)
        c_ref[i, 0:8] = here
        c_ref[i, 8:16] = jnp.concatenate(
            [
                jnp.sum(side[0:4], axis=0, keepdims=True),
                jnp.sum(side[4:8], axis=0, keepdims=True),
                kappa_lanes,
                jnp.zeros((5, LANES), F32),
            ],
            axis=0,
        )
        c_ref[i, 16:24] = kappa


def analysis_kernel(
    groups, slabs, ep_ref, r_ref, low_ref, high_ref, c_ref, low_c_ref, high_c_ref, rm_ref,
    y_ref, x0, hx, hs, x1, bg, dev, wts, rc_ref
):
    members = 4 * groups
    slab = lax.axis_index("slab")
    row = slab // ROWS
    has_low = row > 0
    has_high = row < slabs // ROWS - 1
    lane = lane_ids(members)
    lane1 = lane_ids(1)

    rc_ref[0] = low_c_ref[...]
    rc_ref[9] = high_c_ref[...]
    for s in range(8):
        rc_ref[s + 1] = c_ref[s]

    def coefs(s, ce, cn, kappa):
        east = kappa - 0.5 * ce
        west = kappa + 0.5 * ce
        north = kappa - 0.5 * cn
        south = kappa + 0.5 * cn
        return 1.0 - 4.0 * kappa, east, west, north, south

    def outside(s):
        return ((s == 0) & jnp.logical_not(has_low)) | ((s == 9) & jnp.logical_not(has_high))

    def load(s, read, gone):
        def whole(k):
            x = read(k).astype(F32).reshape(members, LANES)
            return x if gone is None else jnp.where(gone, 0.0, x)

        edge = whole(8)
        for k in range(8):
            x = whole(k)
            x0[s * 8 + k] = x
            own = pltpu.roll(x, 8 * k + 5, 1)
            edge = jnp.where((lane == 8 * k + 4) | (lane == 8 * k + 5), own, edge)
        hs[s] = edge

    def load_own(s, carry):
        load(s, lambda k: r_ref[:, s - 1, k], None)
        return carry

    load(0, lambda k: low_ref[:, k], jnp.logical_not(has_low))
    lax.fori_loop(1, 9, load_own, 0)
    load(9, lambda k: high_ref[:, k], jnp.logical_not(has_high))
    half = lane < 64
    packed = [jnp.where(half, hs[2 * q], pltpu.roll(hs[2 * q + 1], 64, 1)) for q in range(5)]

    def pair(a, b):
        return jnp.where(lane1 < 64, a, pltpu.roll(b, 64, 1))

    def swap(x):
        return jnp.where(lax.rem(lane, 8) == 1, pltpu.roll(x, LANES - 1, 1), pltpu.roll(x, 1, 1))

    for q in range(5):
        hx[q] = swap(packed[q])
    stepped = []
    for q in range(5):
        x = packed[q]
        nxt = packed[min(q + 1, 4)]
        prv = packed[max(q - 1, 0)]
        north = jnp.where(lane < 96, pltpu.roll(x, 96, 1), pltpu.roll(nxt, 96, 1))
        south = jnp.where(lane >= 32, pltpu.roll(x, 32, 1), pltpu.roll(prv, 32, 1))
        low = lax.rem(lane, 8) == 1
        east = jnp.where(low, pltpu.roll(x, LANES - 4, 1), pltpu.roll(x, LANES - 1, 1))
        west = jnp.where(low, pltpu.roll(x, 1, 1), pltpu.roll(x, LANES - 2, 1))
        both = [pair(rc_ref[2 * q, 8 + n : 9 + n], rc_ref[2 * q + 1, 8 + n : 9 + n]) for n in range(3)]
        cc, ke, kw, kn, ks = coefs(0, *both)
        new = x * cc + east * ke + west * kw + north * kn + south * ks
        if q == 0:
            new = jnp.where(half & jnp.logical_not(has_low), 0.0, new)
        if q == 4:
            new = jnp.where(jnp.logical_not(half) & jnp.logical_not(has_high), 0.0, new)
        stepped.append(new)
    for q in range(5):
        hx[5 + q] = swap(stepped[q])

    def advance(src, edge_at, t, s, r, v, offset):
        x = src[t - offset * 4]
        north = src[t + 4 - offset * 4]
        south = src[t - 4 - offset * 4]
        base = lax.rem(t, 16) * 8
        edge = pltpu.roll(hx[edge_at + t // 16], lax.rem(254 - base, LANES), 1)
        west = jnp.where(lane == 0, edge, pltpu.roll(x, 1, 1))
        east = jnp.where(lane == LANES - 1, edge, pltpu.roll(x, LANES - 1, 1))
        ce = rc_ref[s, pl.ds(2 * r + v // 2, 1)]
        cn = rc_ref[s, pl.ds(4 + 2 * r + v // 2, 1)]
        kappa = rc_ref[s, pl.ds(16 + 4 * r + v, 1)]
        cc, ke, kw, kn, ks = coefs(0, ce, cn, kappa)
        return x * cc + east * ke + west * kw + north * kn + south * ks

    def first(n, carry):
        s = n // 2
        r = lax.rem(n, 2)
        gone = outside(s)
        for v in range(4):
            new = advance(x0, 0, n * 4 + v, s, r, v, 0)
            x1[n * 4 + v - 4] = jnp.where(gone, 0.0, new)
        return carry

    lax.fori_loop(1, 19, first, 0)

    lane8 = lane_ids(8)
    obs = []
    for a in range(8):
        tile = jnp.zeros((8, LANES), F32)
        for q in range(8):
            tile = jnp.where(lane8 // 16 == q, pltpu.roll(rm_ref[q, 0], (16 * (q - a)) % LANES, 1), tile)
        obs.append(tile)
    root_w = []
    for h in range(2):
        tile = jnp.zeros((8, LANES), F32)
        for q in range(8):
            tile = jnp.where(lane8 // 16 == q, pltpu.roll(rm_ref[q, 1], (16 * (q - h)) % LANES, 1), tile)
        root_w.append(tile)

    spare = jnp.zeros((PAD - members - 1, LANES), BF16)
    for c in range(8):
        for r in range(2):
            rho = 2 * c + r
            for v in range(4):
                t = (rho + 2) * 4 + v
                new = advance(x1, 5, t, c + 1, r, v, 1)
                rounded = new.astype(BF16)
                back = rounded.astype(F32)
                k = r * 4 + v
                at = slice(k * LANES, (k + 1) * LANES)
                bg[c, :, at] = rounded
                average = jnp.sum(back, axis=0, keepdims=True) * (1.0 / members)
                scale = root_w[rho // 8][rho % 8 : rho % 8 + 1] * ep_ref[v]
                tt = rho * 4 + v
                misfit = (obs[tt // 8][tt % 8 : tt % 8 + 1] - average) * scale
                dev[c, 0:members, at] = ((back - average) * scale).astype(BF16)
                dev[c, members:PAD, at] = jnp.concatenate(
                    [misfit, jnp.zeros((PAD - members - 1, LANES), F32)], axis=0
                ).astype(BF16)

    wide = lax.broadcasted_iota(jnp.int32, (PAD, 8 * LANES), 1)
    strip_of = lax.rem(wide, LANES) // 16

    def gram(c, acc):
        a = dev[c]
        zero = jnp.zeros_like(a)
        stack = jnp.concatenate([jnp.where(strip_of == p, a, zero) for p in range(8)], axis=0)
        return acc + lax.dot_general(stack, a, (((1,), (1,)), ((), ())), preferred_element_type=F32)

    grams = lax.fori_loop(0, 8, gram, jnp.zeros((8 * PAD, PAD), F32))

    si = lax.broadcasted_iota(jnp.int32, (PAD, PAD), 0)
    li = lax.broadcasted_iota(jnp.int32, (PAD, PAD), 1)
    inside = (si < members) & (li < members)
    eye = jnp.where((si == li) & inside, 1.0, 0.0)
    dot = functools.partial(jnp.dot, preferred_element_type=F32, precision=lax.Precision.HIGHEST)
    zs, ys, traces = [], [], []
    for p in range(8):
        full = grams[p * PAD : (p + 1) * PAD]
        system = jnp.where(inside, full, 0.0) + (members - 1.0) * eye
        trace = jnp.sum(jnp.sum(system * eye, axis=1, keepdims=True), axis=0, keepdims=True)
        traces.append(trace)
        ys.append(system / trace)
        zs.append(eye)
    for sweep in range(NS_ITERS):
        cs = []
        for p in range(8):
            zy = ys[p] if sweep == 0 else dot(zs[p], ys[p])
            cs.append(1.5 * eye - 0.5 * zy)
        for p in range(8):
            if sweep < NS_ITERS - 1:
                ys[p] = dot(ys[p], cs[p])
            zs[p] = cs[p] if sweep == 0 else dot(cs[p], zs[p])
    heads, tails = [], []
    for p in range(8):
        full = grams[p * PAD : (p + 1) * PAD]
        root = zs[p] / jnp.sqrt(traces[p])
        drive = jnp.where(li[0:1] < members, full[members : members + 1], 0.0)
        first_col = jnp.sum(root * drive, axis=1, keepdims=True)
        mean_row = jnp.sum(root * first_col, axis=0, keepdims=True)
        w = math.sqrt(members - 1.0) * root + mean_row
        total = jnp.sum(w, axis=1, keepdims=True)
        w = jnp.where(inside, w + (1.0 - total) * (1.0 / members), 0.0)[0:members]
        head = w.astype(BF16)
        heads.append(head.astype(F32))
        tails.append(w - head.astype(F32))
    wts[0:members] = jnp.concatenate(heads, axis=1).astype(BF16)
    wts[members : 2 * members] = jnp.concatenate(tails, axis=1).astype(BF16)

    wide2 = lax.broadcasted_iota(jnp.int32, (members, 2 * LANES), 1)
    strip2 = lax.rem(wide2, LANES) // 16
    fill = jnp.zeros((PAD - members, 2 * LANES), BF16)

    def combine(c, carry):
        for pair_at in range(4):
            b = bg[c, :, pair_at * 2 * LANES : (pair_at + 1) * 2 * LANES]
            zero = jnp.zeros_like(b)
            parts = []
            for p in range(8):
                parts += [jnp.where(strip2 == p, b, zero), fill]
            stack = jnp.concatenate(parts, axis=0)
            out = jnp.dot(wts[...], stack, preferred_element_type=F32)
            out = out[0:members] + out[members : 2 * members]
            for k in range(2):
                y_ref[:, c, pair_at * 2 + k] = (
                    out[:, k * LANES : (k + 1) * LANES].reshape(groups, 4, LANES).astype(BF16)
                )
        return carry

    lax.fori_loop(0, 8, combine, 0)


def unpack_kernel(o_ref, out_ref):
    def one(b, carry):
        at = pl.ds(pl.multiple_of(b * LANES, LANES), LANES)
        for r in range(2):
            x = [o_ref[b, r * 4 + v].astype(F32) for v in range(4)]
            for m in range(4):
                out_ref[m, r, :, at] = jnp.concatenate(
                    [x[v][m : m + 1] for v in range(4)], axis=0
                ).astype(BF16)
        return carry

    lax.fori_loop(0, o_ref.shape[0], one, 0)


def on_device(
    initial_samples,
    courant_east,
    northward_courant,
    diffusivity,
    profile_index,
    observations,
    error_precision,
    localization,
    patch_tiles,
    patch_counts,
):
    slabs = lax.axis_size("slab")
    groups = lax.axis_size("grp")
    blocks = ROWS * groups
    rows = slabs // ROWS
    members = 4 * groups
    vmem = pl.BlockSpec(memory_space=pltpu.VMEM)
    smem = pl.BlockSpec(memory_space=pltpu.SMEM)
    params = pltpu.CompilerParams(vmem_limit_bytes=VMEM_LIMIT)

    sent, courants = pl.pallas_call(
        functools.partial(pack_kernel, groups),
        out_shape=(
            jax.ShapeDtypeStruct((blocks, 9, 4, LANES), BF16),
            jax.ShapeDtypeStruct((ROWS, 24, LANES), F32),
        ),
        in_specs=[smem, smem, vmem, vmem, vmem],
        out_specs=(vmem, vmem),
        compiler_params=params,
        name="pack",
    )(profile_index, diffusivity, initial_samples, courant_east, northward_courant)

    obs = observations.reshape(rows, 8, 8, 16).transpose(0, 2, 1, 3).reshape(rows, 8, LANES)
    tile_hot = patch_tiles == jnp.arange(localization.shape[0], dtype=jnp.int32)[None]
    weight = jnp.sum(jnp.where(tile_hot[:, :, None], localization[None], 0.0), axis=1)
    weight = jnp.where(jnp.arange(PATCH * PATCH, dtype=jnp.int32)[None] < patch_counts, weight, 0.0)
    root = jnp.sqrt(weight).reshape(rows, 2, 8, 16).transpose(0, 2, 1, 3).reshape(rows, 8, 32)
    root = jnp.pad(root, ((0, 0), (0, 0), (0, LANES - 32)))
    notes = jnp.stack([obs, root], axis=1)

    both = ("slab", "grp")
    near = [[(r * ROWS + i) * groups + g for g in range(groups) for i in range(ROWS)] for r in range(rows)]
    slab_near = [[r * ROWS + i for i in range(ROWS)] for r in range(rows)]
    slab_far = [[r * ROWS + i for r in range(rows)] for i in range(ROWS)]
    rise = [(s, s + ROWS) for s in range(slabs - ROWS)]
    fall = [(s + ROWS, s) for s in range(slabs - ROWS)]

    home_of = [
        (f, ((f % 8) * ROWS + (f // 8) % ROWS) * groups + f // (8 * ROWS)) for f in range(slabs * groups)
    ]
    notes = lax.ppermute(notes, both, home_of)
    got_m = lax.all_to_all(notes, "slab", 0, 0, axis_index_groups=slab_far, tiled=True)
    got_c = lax.all_to_all(courants, "slab", 0, 0, axis_index_groups=slab_near, tiled=True)
    low_c = lax.ppermute(got_c[ROWS - 1], "slab", rise)
    high_c = lax.ppermute(got_c[0], "slab", fall)
    got = lax.all_to_all(sent, both, 0, 0, axis_index_groups=near, tiled=True)
    got = got.reshape(groups, ROWS, 9, 4, LANES)
    low = lax.ppermute(got[:, ROWS - 1], "slab", rise)
    high = lax.ppermute(got[:, 0], "slab", fall)

    analysed = pl.pallas_call(
        functools.partial(analysis_kernel, groups, slabs),
        out_shape=jax.ShapeDtypeStruct((groups, ROWS, 8, 4, LANES), BF16),
        in_specs=[smem] + [vmem] * 7,
        out_specs=vmem,
        scratch_shapes=[
            pltpu.VMEM((80, members, LANES), F32),
            pltpu.VMEM((10, members, LANES), F32),
            pltpu.VMEM((10, members, LANES), F32),
            pltpu.VMEM((72, members, LANES), F32),
            pltpu.VMEM((8, members, 8 * LANES), BF16),
            pltpu.VMEM((8, PAD, 8 * LANES), BF16),
            pltpu.VMEM((2 * members, 8 * PAD), BF16),
            pltpu.VMEM((10, 24, LANES), F32),
        ],
        compiler_params=params,
        name="analysis",
    )(jnp.sqrt(error_precision), got, low, high, got_c, low_c, high_c, got_m)

    home = lax.all_to_all(
        analysed.reshape(blocks, 8, 4, LANES), both, 0, 0, axis_index_groups=near, tiled=True
    )

    return pl.pallas_call(
        unpack_kernel,
        out_shape=jax.ShapeDtypeStruct((4, 2, 4, blocks * LANES), BF16),
        in_specs=[vmem],
        out_specs=vmem,
        compiler_params=params,
        name="unpack",
    )(home)


def solution(mesh):
    return jax.shard_map(
        on_device,
        mesh=mesh,
        in_specs=(
            P("grp", "slab", None, None),
            P("slab", None, None),
            P("slab", None, None),
            P(),
            P("slab"),
            P(None, None, ("slab", "grp")),
            P(),
            P(),
            P(None, ("slab", "grp")),
            P(None, ("slab", "grp")),
        ),
        out_specs=P("grp", "slab", None, None),
        check_vma=False,
    )
```

time: 315 us -> 158 us (0.50)
  blocking collectives: 117 us -> 34.8 us
  local copies, waits for them, and re-layouts: 74.4 us -> 7.01 us
  starting transfers between devices: 24.2 us -> 74.3 us
  waiting for transfers between devices: 55.5 us -> 8.76 us
  Pallas kernels: 0 us -> 31.5 us
  matrix products: 28.5 us -> 0 us
  other arithmetic: 10.8 us -> 0.19 us
    all_to_all x3 -> x1, blocking collectives: 117 us -> 34.8 us  [on_device(): lax.all_to_all(analysed.reshape(blocks, 8, 4, LANES), both, 0, 0, axis_in...]
    ppermute x4 -> x5, waiting for transfers between devices: 41.4 us -> 4.77 us  [the longest x1 4.76 us: on_device(): high_c = lax.ppermute(got_c[0], 'slab', fall)]
    pallas_call x0 -> x3, Pallas kernels: none -> 31.5 us  [the longest x1 16.1 us: on_device(): pl.pallas_call(functools.partial(analysis_kernel, groups, slabs), out_sha...]
    dot_general x18 -> x0, matrix products: 28.5 us -> none  [the longest x1 13.3 us: analyse_patches(): jnp.einsum('krcvq,jrcvq->rckj', weighted, deviation, precision=highest)]
    all_to_all x1 -> x3, starting transfers between devices: 5.14 us -> 32 us  [the longest x1 12.6 us: on_device(): got = lax.all_to_all(sent, both, 0, 0, axis_index_groups=near, tiled=True)]
    convert_element_type x3 -> x0, local copies, waits for them, and re-layouts: 23.4 us -> none  [the longest x2 22.3 us: analyse_patches(): states = ensemble.astype(jnp.float32)]
    ppermute x4 -> x5, starting transfers between devices: 19.1 us -> 42.3 us  [the longest x1 16.2 us: on_device(): notes = lax.ppermute(notes, both, home_of)]
    transpose x3 -> x2, local copies, waits for them, and re-layouts: 18.9 us -> 0.08 us  [the longest x1 0.05 us: on_device(): observations.reshape(rows, 8, 8, 16).transpose(0, 2, 1, 3)]
  transfers between devices with their start and end apart: 5 -> 8, of which waited for: 3 -> 2; matrix products, arithmetic and copies ran while one was open for 2% -> 2% of each run, Pallas kernels for 0% -> 0%
where the time goes in v1:
time: 158 us; the launch traced here: 157 us
  starting transfers between devices  74.3 us (47%)
  blocking collectives  34.8 us (22%)
  Pallas kernels  31.5 us (20%)
  waiting for transfers between devices  8.76 us (6%)
  local copies, waits for them, and re-layouts  7.01 us (4%)
    all_to_all x1, blocking collectives, on_device(): lax.all_to_all(analysed.reshape(blocks, 8, 4, LANES), both, 0, 0, axis_in...  34.8 us
    ppermute x1, starting transfers between devices, on_device(): notes = lax.ppermute(notes, both, home_of)  16.2 us
    pallas_call x1, Pallas kernels, on_device(): pl.pallas_call(functools.partial(analysis_kernel, groups, slabs), out_sha...  16.1 us
    ppermute x1, starting transfers between devices, on_device(): low = lax.ppermute(got[:, ROWS - 1], 'slab', rise)  15 us
    all_to_all x1, starting transfers between devices, on_device(): got = lax.all_to_all(sent, both, 0, 0, axis_index_groups=near, tiled=True)  12.6 us
    all_to_all x1, starting transfers between devices, on_device(): lax.all_to_all(notes, 'slab', 0, 0, axis_index_groups=slab_far, tiled=True)  12.6 us
    pallas_call x1, Pallas kernels, on_device(): pl.pallas_call(functools.partial(pack_kernel, groups), out_shape=(jax.Sha...  12.1 us
    all_to_all x1, starting transfers between devices, on_device(): lax.all_to_all(courants, 'slab', 0, 0, axis_index_groups=slab_near, tiled...  6.88 us
  transfers between devices with their start and end apart: 8, of which 2 were waited for; matrix products, arithmetic and copies ran while one was open for 2% of the time, Pallas kernels for 0%

profile of v1, /device:TPU:57, one launch (start us, length us, event | category | flops | bytes accessed | tf_op | source)
XLA Modules:
  0.0 156.8 jit_solution(14401673088373011769)
XLA Ops:
  0.0 1.3 copy.21.diff_ref
  1.3 12.1 %pack.1 = (bf16[96,9,4,128]{3,2,1,0:T(4,128)(2,1)}, f32[8,24,128]{2,1,0:T(8,128)}) custom-call(s32[2]{0:T(128)} %prof_ref.1, f32[8,4]{1,0:T(8,128)} %copy.21.diff_ref, bf16[4,2,4,12288]{3,2,1,0:T(4,128)(2,1)} %x_ref.1, f32[2,2,12288]{2,1,0:T(2,128)} %ce_ref.1, f32[2,2,12288]{2,1,0:T(2,128)} %cn_ref.1), custom_call_target="tpu_custom_call" | custom-call | tf_op jit(solution)/shard_map/pack/pallas_call | solution.py:344
  13.5 12.6 %all-to-all-start = ((bf16[96,9,4,128]{3,2,1,0:T(4,128)(2,1)}), bf16[96,9,4,128]{3,2,1,0:T(4,128)(2,1)S(1)}, u32[]{:S(2)}, u32[]{:S(2)}) async-start(bf16[96,9,4,128]{3,2,1,0:T(4,128)(2,1)} %get-tuple-element.7), calls=%async_computation | async-start | bytes 1769472 | tf_op jit(solution)/shard_map/all_to_all | solution.py:379
  26.1 0.1 copy.25
  26.4 0.6 copy-done.9
  27.3 0.6 copy-done.8
  28.2 16.2 %collective-permute-start.4 = (f32[8,2,8,128]{3,2,1,0:T(8,128)S(1)}, f32[8,2,8,128]{3,2,1,0:T(8,128)}, u32[]{:S(2)}, u32[]{:S(2)}) collective-permute-start(f32[8,2,8,128]{3,2,1,0:T(8,128)S(1)} %pad_maximum_fusion), channel_id=1, source_target_pairs={{0,0},{1,96},{2,192},{3,288},{4,384},{5,480},{6,576},{7,672},{8,12... | collective-permute-start | bytes 196616 | tf_op jit(solution)/shard_map/ppermute | solution.py:374
  44.4 4.0 %all-to-all-done = bf16[96,9,4,128]{3,2,1,0:T(4,128)(2,1)S(1)} async-done(((bf16[96,9,4,128]{3,2,1,0:T(4,128)(2,1)}), bf16[96,9,4,128]{3,2,1,0:T(4,128)(2,1)S(1)}, u32[]{:S(2)}, u32[]{:S(2)}) %all-to-all-start) | async-done | bytes 884768 | tf_op jit(solution)/shard_map/all_to_all | solution.py:379
  48.4 6.9 %all-to-all-start.1 = ((f32[8,24,128]{2,1,0:T(8,128)}), f32[8,24,128]{2,1,0:T(8,128)S(1)}, u32[]{:S(2)}, u32[]{:S(2)}) async-start(f32[8,24,128]{2,1,0:T(8,128)} %get-tuple-element.8), calls=%async_computation.1 | async-start | bytes 196608 | tf_op jit(solution)/shard_map/all_to_all | solution.py:376
  55.2 0.1 copy.34
  55.4 0.3 fusion
  55.8 15.0 %collective-permute-start = (bf16[12,9,4,128]{3,2,1,0:T(4,128)(2,1)S(1)}, bf16[12,9,4,128]{3,2,1,0:T(4,128)(2,1)S(1)}, u32[]{:S(2)}, u32[]{:S(2)}) collective-permute-start(bf16[12,9,4,128]{3,2,1,0:T(4,128)(2,1)S(1)} %bitcast.29), channel_id=1, source_target_pairs={{0,96},{12,108},{24,120},{36,132},{48,144},{60,156},{72,168},{84,1... | collective-permute-start | bytes 331784 | tf_op jit(solution)/shard_map/ppermute | solution.py:381
  70.8 1.9 %collective-permute-start.1 = (bf16[12,9,4,128]{3,2,1,0:T(4,128)(2,1)S(1)}, bf16[12,9,4,128]{3,2,1,0:T(4,128)(2,1)S(1)}, u32[]{:S(2)}, u32[]{:S(2)}) collective-permute-start(bf16[12,9,4,128]{3,2,1,0:T(4,128)(2,1)S(1)} %bitcast.30), channel_id=1, source_target_pairs={{96,0},{108,12},{120,24},{132,36},{144,48},{156,60},{168,72},{180,... | collective-permute-start | bytes 331784 | tf_op jit(solution)/shard_map/ppermute | solution.py:382
  72.8 12.6 %all-to-all-start.2 = ((f32[8,2,8,128]{3,2,1,0:T(8,128)}), f32[8,2,8,128]{3,2,1,0:T(8,128)S(1)}, u32[]{:S(2)}, u32[]{:S(2)}) async-start(f32[8,2,8,128]{3,2,1,0:T(8,128)} %collective-permute-done.4), calls=%async_computation.2 | async-start | bytes 131072 | tf_op jit(solution)/shard_map/all_to_all | solution.py:375
  85.3 4.9 %collective-permute-start.2 = (f32[24,128]{1,0:T(8,128)S(1)}, f32[24,128]{1,0:T(8,128)S(1)}, u32[]{:S(2)}, u32[]{:S(2)}) collective-permute-start(f32[24,128]{1,0:T(8,128)S(1)} %get-tuple-element.12), channel_id=1, source_target_pairs={{0,96},{12,108},{24,120},{36,132},{48,144},{60,156},{72,168},{84,1... | collective-permute-start | bytes 36872 | tf_op jit(solution)/shard_map/ppermute | solution.py:377
  90.2 4.3 %collective-permute-start.3 = (f32[24,128]{1,0:T(8,128)S(1)}, f32[24,128]{1,0:T(8,128)S(1)}, u32[]{:S(2)}, u32[]{:S(2)}) collective-permute-start(f32[24,128]{1,0:T(8,128)S(1)} %get-tuple-element.11), channel_id=1, source_target_pairs={{96,0},{108,12},{120,24},{132,36},{144,48},{156,60},{168,72},{180,... | collective-permute-start | bytes 36872 | tf_op jit(solution)/shard_map/ppermute | solution.py:378
  94.5 0.6 sqrt.7.ep_ref
  95.1 1.4 copy.28.r_ref
  96.5 4.8 %collective-permute-done.3.high_c_ref = f32[24,128]{1,0:T(8,128)S(1)} collective-permute-done((f32[24,128]{1,0:T(8,128)S(1)}, f32[24,128]{1,0:T(8,128)S(1)}, u32[]{:S(2)}, u32[]{:S(2)}) %collective-permute-start.3) | collective-permute-done | bytes 12320 | tf_op jit(solution)/shard_map/ppermute | solution.py:378
  101.3 0.6 copy-done.6
  101.9 0.6 copy-done.3
  102.6 16.1 %analysis.1 = bf16[12,8,8,4,128]{4,3,2,1,0:T(4,128)(2,1)} custom-call(f32[4]{0:T(128)} %sqrt.7.ep_ref, bf16[12,8,9,4,128]{4,3,2,1,0:T(4,128)(2,1)} %copy.28.r_ref, bf16[12,9,4,128]{3,2,1,0:T(4,128)(2,1)} %copy-done.2, bf16[12,9,4,128]{3,2,1,0:T(4,128)(2,1)} %copy-done.3, f32[8,24,128]{2,1,0:T(8,128)} %copy-done, f32[24,128]{1,0:T(8,128)} %copy-done.5, ...), custom_call_target="tpu_custom_call" | custom-call | tf_op jit(solution)/shard_map/analysis/pallas_call | solution.py:384
  118.7 34.8 %all_to_all.20.o_ref = bf16[96,8,4,128]{3,2,1,0:T(4,128)(2,1)} all-to-all(bf16[96,8,4,128]{3,2,1,0:T(4,128)(2,1)} %bitcast.27), channel_id=1, replica_groups={{0,12,24,36,48,60,72,84,1,13,25,37,49,61,73,85,2,14,26,38,50,62,74,86,3..., dimensions={0} | all-to-all | bytes 1572864 | tf_op jit(solution)/shard_map/all_to_all | solution.py:403
  153.4 3.3 %unpack.1 = bf16[4,2,4,12288]{3,2,1,0:T(4,128)(2,1)} custom-call(bf16[96,8,4,128]{3,2,1,0:T(4,128)(2,1)} %all_to_all.20.o_ref), custom_call_target="tpu_custom_call" | custom-call | tf_op jit(solution)/shard_map/unpack/pallas_call | solution.py:407
  (38 shorter events, 0.8 us)
Async XLA Ops:
  13.5 12.6 %copy-start.4 = (f32[128,4,16]{0,2,1:T(8,128)S(1)}, f32[128,4,16]{0,2,1:T(8,128)}, u32[]{:S(2)}) copy-start(f32[128,4,16]{0,2,1:T(8,128)} %param.15) | copy-start | bytes 98308
  13.5 34.9 %all-to-all-start = ((bf16[96,9,4,128]{3,2,1,0:T(4,128)(2,1)}), bf16[96,9,4,128]{3,2,1,0:T(4,128)(2,1)S(1)}, u32[]{:S(2)}, u32[]{:S(2)}) async-start(bf16[96,9,4,128]{3,2,1,0:T(4,128)(2,1)} %get-tuple-element.7), calls=%async_computation | async-start | bytes 1769472 | tf_op jit(solution)/shard_map/all_to_all | solution.py:379
  26.3 0.8 copy-start.7
  26.4 0.7 copy-start.9
  27.3 0.7 copy-start.8
  28.2 44.6 %collective-permute-start.4 = (f32[8,2,8,128]{3,2,1,0:T(8,128)S(1)}, f32[8,2,8,128]{3,2,1,0:T(8,128)}, u32[]{:S(2)}, u32[]{:S(2)}) collective-permute-start(f32[8,2,8,128]{3,2,1,0:T(8,128)S(1)} %pad_maximum_fusion), channel_id=1, source_target_pairs={{0,0},{1,96},{2,192},{3,288},{4,384},{5,480},{6,576},{7,672},{8,12... | collective-permute-start | bytes 196616 | tf_op jit(solution)/shard_map/ppermute | solution.py:374
  48.4 24.4 %all-to-all-start.1 = ((f32[8,24,128]{2,1,0:T(8,128)}), f32[8,24,128]{2,1,0:T(8,128)S(1)}, u32[]{:S(2)}, u32[]{:S(2)}) async-start(f32[8,24,128]{2,1,0:T(8,128)} %get-tuple-element.8), calls=%async_computation.1 | async-start | bytes 196608 | tf_op jit(solution)/shard_map/all_to_all | solution.py:376
  55.8 45.5 %collective-permute-start = (bf16[12,9,4,128]{3,2,1,0:T(4,128)(2,1)S(1)}, bf16[12,9,4,128]{3,2,1,0:T(4,128)(2,1)S(1)}, u32[]{:S(2)}, u32[]{:S(2)}) collective-permute-start(bf16[12,9,4,128]{3,2,1,0:T(4,128)(2,1)S(1)} %bitcast.29), channel_id=1, source_target_pairs={{0,96},{12,108},{24,120},{36,132},{48,144},{60,156},{72,168},{84,1... | collective-permute-start | bytes 331784 | tf_op jit(solution)/shard_map/ppermute | solution.py:381
  70.8 30.5 %collective-permute-start.1 = (bf16[12,9,4,128]{3,2,1,0:T(4,128)(2,1)S(1)}, bf16[12,9,4,128]{3,2,1,0:T(4,128)(2,1)S(1)}, u32[]{:S(2)}, u32[]{:S(2)}) collective-permute-start(bf16[12,9,4,128]{3,2,1,0:T(4,128)(2,1)S(1)} %bitcast.30), channel_id=1, source_target_pairs={{96,0},{108,12},{120,24},{132,36},{144,48},{156,60},{168,72},{180,... | collective-permute-start | bytes 331784 | tf_op jit(solution)/shard_map/ppermute | solution.py:382
  72.7 23.8 %copy-start = (f32[8,24,128]{2,1,0:T(8,128)}, f32[8,24,128]{2,1,0:T(8,128)S(1)}, u32[]{:S(2)}) copy-start(f32[8,24,128]{2,1,0:T(8,128)S(1)} %all-to-all-done.1.c_ref) | copy-start | bytes 294916
  72.8 28.5 %all-to-all-start.2 = ((f32[8,2,8,128]{3,2,1,0:T(8,128)}), f32[8,2,8,128]{3,2,1,0:T(8,128)S(1)}, u32[]{:S(2)}, u32[]{:S(2)}) async-start(f32[8,2,8,128]{3,2,1,0:T(8,128)} %collective-permute-done.4), calls=%async_computation.2 | async-start | bytes 131072 | tf_op jit(solution)/shard_map/all_to_all | solution.py:375
  85.3 9.2 %copy-start.10 = (f32[4]{0:T(128)S(1)}, f32[4]{0:T(128)}, u32[]{:S(2)}) copy-start(f32[4]{0:T(128)} %param.16) | copy-start | bytes 52
  85.3 11.2 %collective-permute-start.2 = (f32[24,128]{1,0:T(8,128)S(1)}, f32[24,128]{1,0:T(8,128)S(1)}, u32[]{:S(2)}, u32[]{:S(2)}) collective-permute-start(f32[24,128]{1,0:T(8,128)S(1)} %get-tuple-element.12), channel_id=1, source_target_pairs={{0,96},{12,108},{24,120},{36,132},{48,144},{60,156},{72,168},{84,1... | collective-permute-start | bytes 36872 | tf_op jit(solution)/shard_map/ppermute | solution.py:377
  90.2 11.0 %collective-permute-start.3 = (f32[24,128]{1,0:T(8,128)S(1)}, f32[24,128]{1,0:T(8,128)S(1)}, u32[]{:S(2)}, u32[]{:S(2)}) collective-permute-start(f32[24,128]{1,0:T(8,128)S(1)} %get-tuple-element.11), channel_id=1, source_target_pairs={{96,0},{108,12},{120,24},{132,36},{144,48},{156,60},{168,72},{180,... | collective-permute-start | bytes 36872 | tf_op jit(solution)/shard_map/ppermute | solution.py:378
  96.5 4.8 %copy-start.5 = (f32[24,128]{1,0:T(8,128)}, f32[24,128]{1,0:T(8,128)S(1)}, u32[]{:S(2)}) copy-start(f32[24,128]{1,0:T(8,128)S(1)} %collective-permute-done.2.low_c_ref) | copy-start | bytes 36868
  101.3 0.6 copy-start.6
  101.3 0.6 copy-start.1
  101.3 0.7 copy-start.2
  101.9 0.7 copy-start.3

commit v2 on v1

--- a/solution.py
+++ b/solution.py
@@ -22,26 +22,25 @@
     return lax.broadcasted_iota(jnp.int32, (rows, LANES), 1)
 
 
-def pack_kernel(groups, prof_ref, diff_ref, x_ref, ce_ref, cn_ref, s_ref, c_ref):
+def pack_kernel(groups, prof_ref, diff_ref, x_ref, ce_ref, cn_ref, s_ref):
     blocks = ROWS * groups
     me = lax.axis_index("grp")
+    part = lax.rem(me // 4, 3)
+    kind = lax.rem(me, 4)
     lane4 = lane_ids(4)
 
-    def tiles(b):
-        at = pl.ds(pl.multiple_of(b * LANES, LANES), LANES)
-        return [[x_ref[m, r, :, at].astype(F32) for r in range(2)] for m in range(4)]
-
-    def turned(x, r, v):
-        return jnp.concatenate([x[m][r][v : v + 1] for m in range(4)], axis=0)
+    def place(b):
+        return pl.ds(pl.multiple_of(b * LANES, LANES), LANES)
 
     def one(b, carry):
-        x = tiles(b)
+        at = place(b)
         for r in range(2):
+            x = [x_ref[m, r, :, at].astype(F32) for m in range(4)]
             for v in range(4):
-                s_ref[b, r * 4 + v] = turned(x, r, v).astype(BF16)
-        return carry
-
-    lax.fori_loop(0, blocks, one, 0)
+                s_ref[b, r * 4 + v] = jnp.concatenate([x[m][v : v + 1] for m in range(4)], axis=0).astype(BF16)
+        return carry
+
+    lax.fori_loop(0, blocks, one, 0, unroll=4)
 
     def edges(b, carry):
         before = lax.rem(b + blocks - 1, blocks)
@@ -54,49 +53,83 @@
         s_ref[b, 8] = packed.astype(BF16)
         return carry
 
-    lax.fori_loop(0, blocks, edges, 0)
-
-    kappas = []
-    for r in range(2):
-        for v in range(4):
-            kappas.append(jnp.full((1, LANES), diff_ref[prof_ref[r], v], F32))
-    kappa = jnp.concatenate(kappas, axis=0)
-    lane1 = lane_ids(1)
-    kappa_lanes = jnp.zeros((1, LANES), F32)
-    for k in range(8):
-        kappa_lanes = jnp.where(lane1 // 8 == k, kappas[k], kappa_lanes)
-
-    lane8 = lane_ids(8)
-    sub8 = lax.broadcasted_iota(jnp.int32, (8, LANES), 0)
-    mine = (lax.rem(sub8, 4) == lane8 // 16) & (lane8 < 64)
-
-    def courant(b):
-        at = pl.ds(pl.multiple_of(b * LANES, LANES), LANES)
-        return jnp.concatenate([ce_ref[0, :, at], ce_ref[1, :, at], cn_ref[0, :, at], cn_ref[1, :, at]], axis=0)
-
-    for i in range(ROWS):
-        b = me * ROWS + i
-        here = courant(b)
-        before = courant(lax.rem(b + blocks - 1, blocks))
-        after = courant(lax.rem(b + 1, blocks))
-        low = jnp.broadcast_to(before[:, LANES - 1 : LANES], (8, LANES))
-        high = jnp.broadcast_to(after[:, 0:1], (8, LANES))
-        side = jnp.where(mine, jnp.where(lax.rem(lane8, 8) == 1, low, high), 0.0)
-        c_ref[i, 0:8] = here
-        c_ref[i, 8:16] = jnp.concatenate(
-            [
-                jnp.sum(side[0:4], axis=0, keepdims=True),
-                jnp.sum(side[4:8], axis=0, keepdims=True),
-                kappa_lanes,
-                jnp.zeros((5, LANES), F32),
-            ],
-            axis=0,
-        )
-        c_ref[i, 16:24] = kappa
+    lax.fori_loop(0, blocks, edges, 0, unroll=4)
+
+    def term(x):
+        high = x.astype(BF16).astype(F32)
+        rest = x - high
+        middle = rest.astype(BF16).astype(F32)
+        return jnp.where(part == 0, high, jnp.where(part == 1, middle, rest - middle)).astype(BF16)
+
+    def whole(ref, at):
+        return jnp.concatenate([ref[0, :, at], ref[1, :, at]], axis=0)
+
+    def plain(ref):
+        def go(b, carry):
+            s_ref[b, 9] = term(whole(ref, place(b)))
+            return carry
+
+        lax.fori_loop(0, blocks, go, 0, unroll=4)
+
+    @pl.when(kind == 0)
+    def _():
+        plain(ce_ref)
+
+    @pl.when(kind == 1)
+    def _():
+        plain(cn_ref)
+
+    @pl.when(kind == 2)
+    def _():
+        lane1 = lane_ids(1)
+        kappa_lanes = jnp.zeros((1, LANES), F32)
+        for k in range(8):
+            value = diff_ref[prof_ref[k // 4], k % 4]
+            kappa_lanes = jnp.where(lane1 // 8 == k, value, kappa_lanes)
+        sub4 = lax.broadcasted_iota(jnp.int32, (4, LANES), 0)
+        mine = (sub4 == lane4 // 16) & (lane4 < 64)
+        low_at = lax.rem(lane4, 8) == 1
+
+        def go(b, carry):
+            before = place(lax.rem(b + blocks - 1, blocks))
+            after = place(lax.rem(b + 1, blocks))
+            rows = []
+            for ref in (ce_ref, cn_ref):
+                low = jnp.broadcast_to(whole(ref, before)[:, LANES - 1 : LANES], (4, LANES))
+                high = jnp.broadcast_to(whole(ref, after)[:, 0:1], (4, LANES))
+                side = jnp.where(mine, jnp.where(low_at, low, high), 0.0)
+                rows.append(jnp.sum(side, axis=0, keepdims=True))
+            s_ref[b, 9] = term(jnp.concatenate(rows + [kappa_lanes, jnp.zeros((1, LANES), F32)], axis=0))
+            return carry
+
+        lax.fori_loop(0, blocks, go, 0, unroll=4)
+
+    @pl.when(kind == 3)
+    def _():
+        def go(b, carry):
+            s_ref[b, 9] = jnp.zeros((4, LANES), BF16)
+            return carry
+
+        lax.fori_loop(0, blocks, go, 0, unroll=4)
+
+
+def spread_kernel(n_ref, o_ref):
+    q = lax.axis_index("slab") // ROWS
+    lane = lane_ids(8)
+    mine = lane // 16 == q
+
+    def go(row, carry):
+        for a in range(10):
+            k = a // 8
+            shift = lax.rem(16 * (q + 8 - a % 8), LANES)
+            o_ref[row, a] = jnp.where(mine, pltpu.roll(n_ref[row, k], shift, 1), 0.0)
+        return carry
+
+    lax.fori_loop(0, n_ref.shape[0], go, 0)
 
 
 def analysis_kernel(
-    groups, slabs, ep_ref, r_ref, low_ref, high_ref, c_ref, low_c_ref, high_c_ref, rm_ref,
+    groups, slabs, ep_ref, r_ref, low_ref, high_ref, rm_ref,
     y_ref, x0, hx, hs, x1, bg, dev, wts, rc_ref
 ):
     members = 4 * groups
@@ -107,10 +140,6 @@
     lane = lane_ids(members)
     lane1 = lane_ids(1)
 
-    rc_ref[0] = low_c_ref[...]
-    rc_ref[9] = high_c_ref[...]
-    for s in range(8):
-        rc_ref[s + 1] = c_ref[s]
 
     def coefs(s, ce, cn, kappa):
         east = kappa - 0.5 * ce
@@ -134,13 +163,19 @@
             own = pltpu.roll(x, 8 * k + 5, 1)
             edge = jnp.where((lane == 8 * k + 4) | (lane == 8 * k + 5), own, edge)
         hs[s] = edge
+        rows = whole(9)
+        rows = rows[0:16] + rows[16:32] + rows[32:48]
+        rc_ref[s, 0:16] = rows
+        rc_ref[s, 16:24] = jnp.concatenate(
+            [jnp.broadcast_to(rows[10:11, 8 * k : 8 * k + 1], (1, LANES)) for k in range(8)], axis=0
+        )
 
     def load_own(s, carry):
         load(s, lambda k: r_ref[:, s - 1, k], None)
         return carry
 
     load(0, lambda k: low_ref[:, k], jnp.logical_not(has_low))
-    lax.fori_loop(1, 9, load_own, 0)
+    lax.fori_loop(1, 9, load_own, 0, unroll=2)
     load(9, lambda k: high_ref[:, k], jnp.logical_not(has_high))
     half = lane < 64
     packed = [jnp.where(half, hs[2 * q], pltpu.roll(hs[2 * q + 1], 64, 1)) for q in range(5)]
@@ -197,23 +232,11 @@
             x1[n * 4 + v - 4] = jnp.where(gone, 0.0, new)
         return carry
 
-    lax.fori_loop(1, 19, first, 0)
-
-    lane8 = lane_ids(8)
-    obs = []
-    for a in range(8):
-        tile = jnp.zeros((8, LANES), F32)
-        for q in range(8):
-            tile = jnp.where(lane8 // 16 == q, pltpu.roll(rm_ref[q, 0], (16 * (q - a)) % LANES, 1), tile)
-        obs.append(tile)
-    root_w = []
-    for h in range(2):
-        tile = jnp.zeros((8, LANES), F32)
-        for q in range(8):
-            tile = jnp.where(lane8 // 16 == q, pltpu.roll(rm_ref[q, 1], (16 * (q - h)) % LANES, 1), tile)
-        root_w.append(tile)
-
-    spare = jnp.zeros((PAD - members - 1, LANES), BF16)
+    lax.fori_loop(1, 19, first, 0, unroll=2)
+
+    obs = [rm_ref[a] for a in range(8)]
+    root_w = [rm_ref[8 + h] for h in range(2)]
+
     for c in range(8):
         for r in range(2):
             rho = 2 * c + r
@@ -341,14 +364,11 @@
     smem = pl.BlockSpec(memory_space=pltpu.SMEM)
     params = pltpu.CompilerParams(vmem_limit_bytes=VMEM_LIMIT)
 
-    sent, courants = pl.pallas_call(
+    sent = pl.pallas_call(
         functools.partial(pack_kernel, groups),
-        out_shape=(
-            jax.ShapeDtypeStruct((blocks, 9, 4, LANES), BF16),
-            jax.ShapeDtypeStruct((ROWS, 24, LANES), F32),
-        ),
+        out_shape=jax.ShapeDtypeStruct((blocks, 10, 4, LANES), BF16),
         in_specs=[smem, smem, vmem, vmem, vmem],
-        out_specs=(vmem, vmem),
+        out_specs=vmem,
         compiler_params=params,
         name="pack",
     )(profile_index, diffusivity, initial_samples, courant_east, northward_courant)
@@ -363,7 +383,6 @@
 
     both = ("slab", "grp")
     near = [[(r * ROWS + i) * groups + g for g in range(groups) for i in range(ROWS)] for r in range(rows)]
-    slab_near = [[r * ROWS + i for i in range(ROWS)] for r in range(rows)]
     slab_far = [[r * ROWS + i for r in range(rows)] for i in range(ROWS)]
     rise = [(s, s + ROWS) for s in range(slabs - ROWS)]
     fall = [(s + ROWS, s) for s in range(slabs - ROWS)]
@@ -372,19 +391,26 @@
         (f, ((f % 8) * ROWS + (f // 8) % ROWS) * groups + f // (8 * ROWS)) for f in range(slabs * groups)
     ]
     notes = lax.ppermute(notes, both, home_of)
-    got_m = lax.all_to_all(notes, "slab", 0, 0, axis_index_groups=slab_far, tiled=True)
-    got_c = lax.all_to_all(courants, "slab", 0, 0, axis_index_groups=slab_near, tiled=True)
-    low_c = lax.ppermute(got_c[ROWS - 1], "slab", rise)
-    high_c = lax.ppermute(got_c[0], "slab", fall)
+    spread = pl.pallas_call(
+        spread_kernel,
+        out_shape=jax.ShapeDtypeStruct((rows, 10, 8, LANES), F32),
+        in_specs=[vmem],
+        out_specs=vmem,
+        compiler_params=params,
+        name="spread",
+    )(notes)
+    sent, spread = lax.optimization_barrier((sent, spread))
+    got_m = lax.psum_scatter(spread, "slab", scatter_dimension=0, axis_index_groups=slab_far)
+
     got = lax.all_to_all(sent, both, 0, 0, axis_index_groups=near, tiled=True)
-    got = got.reshape(groups, ROWS, 9, 4, LANES)
+    got = got.reshape(groups, ROWS, 10, 4, LANES)
     low = lax.ppermute(got[:, ROWS - 1], "slab", rise)
     high = lax.ppermute(got[:, 0], "slab", fall)
 
     analysed = pl.pallas_call(
         functools.partial(analysis_kernel, groups, slabs),
         out_shape=jax.ShapeDtypeStruct((groups, ROWS, 8, 4, LANES), BF16),
-        in_specs=[smem] + [vmem] * 7,
+        in_specs=[smem] + [vmem] * 4,
         out_specs=vmem,
         scratch_shapes=[
             pltpu.VMEM((80, members, LANES), F32),
@@ -398,7 +424,7 @@
         ],
         compiler_params=params,
         name="analysis",
-    )(jnp.sqrt(error_precision), got, low, high, got_c, low_c, high_c, got_m)
+    )(jnp.sqrt(error_precision), got, low, high, got_m)
 
     home = lax.all_to_all(
         analysed.reshape(blocks, 8, 4, LANES), both, 0, 0, axis_index_groups=near, tiled=True

time: 158 us -> 223 us (1.41); the launches traced: 157 us -> 219 us
  waiting for transfers between devices: 8.76 us -> 97.3 us
  starting transfers between devices: 74.3 us -> 36.9 us
  between operations: 0.24 us -> 13.6 us
  blocking collectives: 34.8 us -> 31.8 us
    reduce_scatter x0 -> x1, waiting for transfers between devices: none -> 72.9 us  [on_device(): lax.psum_scatter(spread, 'slab', scatter_dimension=0, axis_index_groups=s...]
    all_to_all x1, waiting for transfers between devices: 3.99 us -> 23.7 us  [on_device(): got = lax.all_to_all(sent, both, 0, 0, axis_index_groups=near, tiled=True)]
    all_to_all x2 -> x0, starting transfers between devices: 19.4 us -> none  [the longest x1 12.6 us: on_device(): lax.all_to_all(notes, 'slab', 0, 0, axis_index_groups=slab_far, tiled=True)]
    ppermute x2 -> x0, starting transfers between devices: 9.19 us -> none  [the longest x1 4.89 us: on_device(): low_c = lax.ppermute(got_c[ROWS - 1], 'slab', rise)]
    ppermute x1, starting transfers between devices: 15 us -> 6.79 us  [on_device(): low = lax.ppermute(got[:, ROWS - 1], 'slab', rise)]
    ppermute x2 -> x0, waiting for transfers between devices: 4.76 us -> none  [the longest x1 4.76 us: on_device(): high_c = lax.ppermute(got_c[0], 'slab', fall)]
    all_to_all x1, blocking collectives: 34.8 us -> 31.8 us  [on_device(): lax.all_to_all(analysed.reshape(blocks, 8, 4, LANES), both, 0, 0, axis_in...]
    pallas_call x1 -> x2, Pallas kernels: 12.1 us -> 13.6 us  [the longest x1 11.4 us: on_device(): pl.pallas_call(functools.partial(pack_kernel, groups), out_shape=jax.Shap...]
  transfers between devices with their start and end apart: 8 -> 5, of which waited for: 2 -> 2; matrix products, arithmetic and copies ran while one was open for 2% -> 2% of each run, Pallas kernels for 0% -> 5%
where the time goes in v2:
time: 223 us; the launch traced here: 219 us
  waiting for transfers between devices  97.3 us (44%)
  starting transfers between devices  36.9 us (17%)
  Pallas kernels  32 us (14%)
  blocking collectives  31.8 us (14%)
  between operations  13.6 us (6%)
  local copies, waits for them, and re-layouts  7.27 us (3%)
    reduce_scatter x1, waiting for transfers between devices, on_device(): lax.psum_scatter(spread, 'slab', scatter_dimension=0, axis_index_groups=s...  72.9 us
    all_to_all x1, blocking collectives, on_device(): lax.all_to_all(analysed.reshape(blocks, 8, 4, LANES), both, 0, 0, axis_in...  31.8 us
    all_to_all x1, waiting for transfers between devices, on_device(): got = lax.all_to_all(sent, both, 0, 0, axis_index_groups=near, tiled=True)  23.7 us
    ppermute x1, starting transfers between devices, on_device(): notes = lax.ppermute(notes, both, home_of)  17.1 us
    pallas_call x1, Pallas kernels, on_device(): pl.pallas_call(functools.partial(analysis_kernel, groups, slabs), out_sha...  15.1 us
    pallas_call x1, Pallas kernels, on_device(): pl.pallas_call(functools.partial(pack_kernel, groups), out_shape=jax.Shap...  11.4 us
    all_to_all x1, starting transfers between devices, on_device(): got = lax.all_to_all(sent, both, 0, 0, axis_index_groups=near, tiled=True)  10.6 us
    ppermute x1, starting transfers between devices, on_device(): low = lax.ppermute(got[:, ROWS - 1], 'slab', rise)  6.79 us
  transfers between devices with their start and end apart: 5, of which 2 were waited for; matrix products, arithmetic and copies ran while one was open for 2% of the time, Pallas kernels for 5%

profile of v2, /device:TPU:57, one launch (start us, length us, event | category | flops | bytes accessed | tf_op | source)
XLA Modules:
  0.0 219.0 jit_solution(6100497066904416053)
XLA Ops:
  6.5 0.7 copy-done.7
  7.4 0.6 copy-done.6
  8.3 0.7 copy-done.3
  9.0 0.1 copy.22
  9.2 0.1 stack_reshape.3
  9.4 17.1 %collective-permute-start = (f32[8,2,8,128]{3,2,1,0:T(8,128)S(1)}, f32[8,2,8,128]{3,2,1,0:T(8,128)S(1)}, u32[]{:S(2)}, u32[]{:S(2)}) collective-permute-start(f32[8,2,8,128]{3,2,1,0:T(8,128)S(1)} %pad_maximum_fusion), channel_id=1, source_target_pairs={{0,0},{1,96},{2,192},{3,288},{4,384},{5,480},{6,576},{7,672},{8,12... | collective-permute-start | bytes 196616 | tf_op jit(solution)/shard_map/ppermute | solution.py:393
  26.5 0.7 copy.21.diff_ref
  27.2 11.4 %pack.1 = bf16[96,10,4,128]{3,2,1,0:T(4,128)(2,1)} custom-call(s32[2]{0:T(128)} %prof_ref.1, f32[8,4]{1,0:T(8,128)} %copy.21.diff_ref, bf16[4,2,4,12288]{3,2,1,0:T(4,128)(2,1)} %x_ref.1, f32[2,2,12288]{2,1,0:T(2,128)} %ce_ref.1, f32[2,2,12288]{2,1,0:T(2,128)} %cn_ref.1), custom_call_target="tpu_custom_call" | custom-call | tf_op jit(solution)/shard_map/pack/pallas_call | solution.py:367
  38.5 0.6 copy-done.2
  39.2 2.2 %spread.1 = f32[8,10,8,128]{3,2,1,0:T(8,128)} custom-call(f32[8,2,8,128]{3,2,1,0:T(8,128)} %copy-done.2), custom_call_target="tpu_custom_call" | custom-call | tf_op jit(solution)/shard_map/spread/pallas_call | solution.py:394
  41.4 10.6 %all-to-all-start = ((bf16[96,10,4,128]{3,2,1,0:T(4,128)(2,1)}), bf16[96,10,4,128]{3,2,1,0:T(4,128)(2,1)S(1)}, u32[]{:S(2)}, u32[]{:S(2)}) async-start(bf16[96,10,4,128]{3,2,1,0:T(4,128)(2,1)} %pack.1), calls=%async_computation | async-start | bytes 1966080 | tf_op jit(solution)/shard_map/all_to_all | solution.py:405
  52.1 0.7 reduce-scatter.2.cloned.1.call-update
  52.8 23.7 %all-to-all-done = bf16[96,10,4,128]{3,2,1,0:T(4,128)(2,1)S(1)} async-done(((bf16[96,10,4,128]{3,2,1,0:T(4,128)(2,1)}), bf16[96,10,4,128]{3,2,1,0:T(4,128)(2,1)S(1)}, u32[]{:S(2)}, u32[]{:S(2)}) %all-to-all-start) | async-done | bytes 983072 | tf_op jit(solution)/shard_map/all_to_all | solution.py:405
  76.4 0.2 copy.34
  76.6 0.3 fusion
  77.1 6.8 %collective-permute-start.1 = (bf16[12,10,4,128]{3,2,1,0:T(4,128)(2,1)S(1)}, bf16[12,10,4,128]{3,2,1,0:T(4,128)(2,1)S(1)}, u32[]{:S(2)}, u32[]{:S(2)}) collective-permute-start(bf16[12,10,4,128]{3,2,1,0:T(4,128)(2,1)S(1)} %bitcast.27), channel_id=1, source_target_pairs={{0,96},{12,108},{24,120},{36,132},{48,144},{60,156},{72,168},{84,1... | collective-permute-start | bytes 368648 | tf_op jit(solution)/shard_map/ppermute | solution.py:407
  83.9 2.4 %collective-permute-start.2 = (bf16[12,10,4,128]{3,2,1,0:T(4,128)(2,1)S(1)}, bf16[12,10,4,128]{3,2,1,0:T(4,128)(2,1)S(1)}, u32[]{:S(2)}, u32[]{:S(2)}) collective-permute-start(bf16[12,10,4,128]{3,2,1,0:T(4,128)(2,1)S(1)} %bitcast.26), channel_id=1, source_target_pairs={{96,0},{108,12},{120,24},{132,36},{144,48},{156,60},{168,72},{180,... | collective-permute-start | bytes 368648 | tf_op jit(solution)/shard_map/ppermute | solution.py:408
  86.3 0.6 sqrt.7.ep_ref
  86.9 1.5 copy.28.r_ref
  88.3 72.9 %reduce-scatter.2.cloned.1.call-done = f32[1,10,8,128]{3,2,1,0:T(8,128)} async-done(((f32[8,10,8,128]{3,2,1,0:T(8,128)}), f32[1,10,8,128]{3,2,1,0:T(8,128)}) %reduce-scatter.2.cloned.1.call-update) | async-done | bytes 40976 | tf_op jit(solution)/shard_map/reduce_scatter | solution.py:403
  161.3 0.6 copy-done
  162.0 15.1 %analysis.1 = bf16[12,8,8,4,128]{4,3,2,1,0:T(4,128)(2,1)} custom-call(f32[4]{0:T(128)} %sqrt.7.ep_ref, bf16[12,8,10,4,128]{4,3,2,1,0:T(4,128)(2,1)} %copy.28.r_ref, bf16[12,10,4,128]{3,2,1,0:T(4,128)(2,1)} %copy-done, bf16[12,10,4,128]{3,2,1,0:T(4,128)(2,1)} %copy-done.1, f32[10,8,128]{2,1,0:T(8,128)} %bitcast.28), custom_call_target="tpu_custom_call" | custom-call | tf_op jit(solution)/shard_map/analysis/pallas_call | solution.py:410
  177.0 31.8 %all_to_all.10.o_ref = bf16[96,8,4,128]{3,2,1,0:T(4,128)(2,1)} all-to-all(bf16[96,8,4,128]{3,2,1,0:T(4,128)(2,1)} %bitcast.24), channel_id=1, replica_groups={{0,12,24,36,48,60,72,84,1,13,25,37,49,61,73,85,2,14,26,38,50,62,74,86,3..., dimensions={0} | all-to-all | bytes 1572864 | tf_op jit(solution)/shard_map/all_to_all | solution.py:429
  208.9 3.3 %unpack.1 = bf16[4,2,4,12288]{3,2,1,0:T(4,128)(2,1)} custom-call(bf16[96,8,4,128]{3,2,1,0:T(4,128)(2,1)} %all_to_all.10.o_ref), custom_call_target="tpu_custom_call" | custom-call | tf_op jit(solution)/shard_map/unpack/pallas_call | solution.py:433
  (29 shorter events, 0.7 us)
Async XLA Ops:
  6.5 0.7 copy-start.4
  6.5 0.7 copy-start.7
  7.4 0.7 copy-start.6
  8.3 0.8 copy-start.3
  9.4 17.1 %copy-start.5 = (f32[8,4]{0,1:T(4,128)S(1)}, f32[8,4]{0,1:T(4,128)}, u32[]{:S(2)}) copy-start(f32[8,4]{0,1:T(4,128)} %param.13) | copy-start | bytes 388
  9.4 29.1 %collective-permute-start = (f32[8,2,8,128]{3,2,1,0:T(8,128)S(1)}, f32[8,2,8,128]{3,2,1,0:T(8,128)S(1)}, u32[]{:S(2)}, u32[]{:S(2)}) collective-permute-start(f32[8,2,8,128]{3,2,1,0:T(8,128)S(1)} %pad_maximum_fusion), channel_id=1, source_target_pairs={{0,0},{1,96},{2,192},{3,288},{4,384},{5,480},{6,576},{7,672},{8,12... | collective-permute-start | bytes 196616 | tf_op jit(solution)/shard_map/ppermute | solution.py:393
  38.5 0.6 copy-start.2
  41.4 35.0 %all-to-all-start = ((bf16[96,10,4,128]{3,2,1,0:T(4,128)(2,1)}), bf16[96,10,4,128]{3,2,1,0:T(4,128)(2,1)S(1)}, u32[]{:S(2)}, u32[]{:S(2)}) async-start(bf16[96,10,4,128]{3,2,1,0:T(4,128)(2,1)} %pack.1), calls=%async_computation | async-start | bytes 1966080 | tf_op jit(solution)/shard_map/all_to_all | solution.py:405
  52.0 109.2 %reduce-scatter.2.cloned.1.call-start = ((), (), s32[]{:S(2)}) async-start(), calls=%async_computation.3 | async-start | bytes 368640 | tf_op jit(solution)/shard_map/reduce_scatter | solution.py:403
  77.1 9.2 %copy-start.8 = (f32[4]{0:T(128)S(1)}, f32[4]{0:T(128)}, u32[]{:S(2)}) copy-start(f32[4]{0:T(128)} %param.16) | copy-start | bytes 52
  77.1 84.2 %collective-permute-start.1 = (bf16[12,10,4,128]{3,2,1,0:T(4,128)(2,1)S(1)}, bf16[12,10,4,128]{3,2,1,0:T(4,128)(2,1)S(1)}, u32[]{:S(2)}, u32[]{:S(2)}) collective-permute-start(bf16[12,10,4,128]{3,2,1,0:T(4,128)(2,1)S(1)} %bitcast.27), channel_id=1, source_target_pairs={{0,96},{12,108},{24,120},{36,132},{48,144},{60,156},{72,168},{84,1... | collective-permute-start | bytes 368648 | tf_op jit(solution)/shard_map/ppermute | solution.py:407
  83.9 77.4 %collective-permute-start.2 = (bf16[12,10,4,128]{3,2,1,0:T(4,128)(2,1)S(1)}, bf16[12,10,4,128]{3,2,1,0:T(4,128)(2,1)S(1)}, u32[]{:S(2)}, u32[]{:S(2)}) collective-permute-start(bf16[12,10,4,128]{3,2,1,0:T(4,128)(2,1)S(1)} %bitcast.26), channel_id=1, source_target_pairs={{96,0},{108,12},{120,24},{132,36},{144,48},{156,60},{168,72},{180,... | collective-permute-start | bytes 368648 | tf_op jit(solution)/shard_map/ppermute | solution.py:408
  161.3 0.7 copy-start
  161.3 0.7 copy-start.1
Sparse Core Ops, SparseCore 0:
  57.8 103.3 reduce-scatter.1

commit v3 on v2

--- a/solution.py
+++ b/solution.py
@@ -22,7 +22,7 @@
     return lax.broadcasted_iota(jnp.int32, (rows, LANES), 1)
 
 
-def pack_kernel(groups, prof_ref, diff_ref, x_ref, ce_ref, cn_ref, s_ref):
+def pack_kernel(groups, prof_ref, diff_ref, x_ref, ce_ref, cn_ref, s_ref, turned):
     blocks = ROWS * groups
     me = lax.axis_index("grp")
     part = lax.rem(me // 4, 3)
@@ -32,12 +32,20 @@
     def place(b):
         return pl.ds(pl.multiple_of(b * LANES, LANES), LANES)
 
+    lane8 = lane_ids(8)
+    sub8 = lax.rem(lax.broadcasted_iota(jnp.int32, (8, LANES), 0), 4)
+
     def one(b, carry):
         at = place(b)
-        for r in range(2):
-            x = [x_ref[m, r, :, at].astype(F32) for m in range(4)]
-            for v in range(4):
-                s_ref[b, r * 4 + v] = jnp.concatenate([x[m][v : v + 1] for m in range(4)], axis=0).astype(BF16)
+        x = [jnp.concatenate([x_ref[m, 0, :, at].astype(F32), x_ref[m, 1, :, at].astype(F32)], axis=0) for m in range(4)]
+        for v in range(4):
+            tile = x[v]
+            for m in range(4):
+                if m != v:
+                    tile = jnp.where(sub8 == m, pltpu.roll(x[m], (m - v) % 8, 0), tile)
+            turned[b, v] = tile
+            s_ref[b, v] = tile[0:4].astype(BF16)
+            s_ref[b, 4 + v] = tile[4:8].astype(BF16)
         return carry
 
     lax.fori_loop(0, blocks, one, 0, unroll=4)
@@ -45,12 +53,13 @@
     def edges(b, carry):
         before = lax.rem(b + blocks - 1, blocks)
         after = lax.rem(b + 1, blocks)
-        packed = jnp.zeros((4, LANES), F32)
-        for k in range(8):
-            mixed = jnp.where(lane4 < 64, s_ref[after, k].astype(F32), s_ref[before, k].astype(F32))
-            moved = pltpu.roll(mixed, 2 + 8 * k, 1)
-            packed = jnp.where((lane4 >= 8 * k) & (lane4 < 8 * k + 4), moved, packed)
-        s_ref[b, 8] = packed.astype(BF16)
+        packed = jnp.zeros((8, LANES), F32)
+        for v in range(4):
+            mixed = jnp.where(lane8 < 64, turned[after, v], turned[before, v])
+            moved = pltpu.roll(mixed, 2 + 8 * v, 1)
+            packed = jnp.where((lane8 >= 8 * v) & (lane8 < 8 * v + 4), moved, packed)
+        packed = packed + pltpu.roll(pltpu.roll(packed, 4, 0), 32, 1)
+        s_ref[b, 8] = packed[0:4].astype(BF16)
         return carry
 
     lax.fori_loop(0, blocks, edges, 0, unroll=4)
@@ -111,21 +120,6 @@
             return carry
 
         lax.fori_loop(0, blocks, go, 0, unroll=4)
-
-
-def spread_kernel(n_ref, o_ref):
-    q = lax.axis_index("slab") // ROWS
-    lane = lane_ids(8)
-    mine = lane // 16 == q
-
-    def go(row, carry):
-        for a in range(10):
-            k = a // 8
-            shift = lax.rem(16 * (q + 8 - a % 8), LANES)
-            o_ref[row, a] = jnp.where(mine, pltpu.roll(n_ref[row, k], shift, 1), 0.0)
-        return carry
-
-    lax.fori_loop(0, n_ref.shape[0], go, 0)
 
 
 def analysis_kernel(
@@ -234,8 +228,13 @@
 
     lax.fori_loop(1, 19, first, 0, unroll=2)
 
-    obs = [rm_ref[a] for a in range(8)]
-    root_w = [rm_ref[8 + h] for h in range(2)]
+    lane8 = lane_ids(8)
+    obs, root_w = [], []
+    for a in range(10):
+        tile = jnp.zeros((8, LANES), F32)
+        for q in range(8):
+            tile = jnp.where(lane8 // 16 == q, pltpu.roll(rm_ref[q, a // 8], (16 * (q - a % 8)) % LANES, 1), tile)
+        (obs if a < 8 else root_w).append(tile)
 
     for c in range(8):
         for r in range(2):
@@ -369,6 +368,7 @@
         out_shape=jax.ShapeDtypeStruct((blocks, 10, 4, LANES), BF16),
         in_specs=[smem, smem, vmem, vmem, vmem],
         out_specs=vmem,
+        scratch_shapes=[pltpu.VMEM((blocks, 4, 8, LANES), F32)],
         compiler_params=params,
         name="pack",
     )(profile_index, diffusivity, initial_samples, courant_east, northward_courant)
@@ -391,17 +391,7 @@
         (f, ((f % 8) * ROWS + (f // 8) % ROWS) * groups + f // (8 * ROWS)) for f in range(slabs * groups)
     ]
     notes = lax.ppermute(notes, both, home_of)
-    spread = pl.pallas_call(
-        spread_kernel,
-        out_shape=jax.ShapeDtypeStruct((rows, 10, 8, LANES), F32),
-        in_specs=[vmem],
-        out_specs=vmem,
-        compiler_params=params,
-        name="spread",
-    )(notes)
-    sent, spread = lax.optimization_barrier((sent, spread))
-    got_m = lax.psum_scatter(spread, "slab", scatter_dimension=0, axis_index_groups=slab_far)
-
+    got_m = lax.all_to_all(notes, "slab", 0, 0, axis_index_groups=slab_far, tiled=True)
     got = lax.all_to_all(sent, both, 0, 0, axis_index_groups=near, tiled=True)
     got = got.reshape(groups, ROWS, 10, 4, LANES)
     low = lax.ppermute(got[:, ROWS - 1], "slab", rise)

time: 223 us -> 144 us (0.65); the launches traced: 219 us -> 144 us
  waiting for transfers between devices: 97.3 us -> 16.9 us
  starting transfers between devices: 36.9 us -> 53.1 us
  between operations: 13.6 us -> 0.19 us
  blocking collectives: 31.8 us -> 40.8 us
  Pallas kernels: 32 us -> 25.9 us
    reduce_scatter x1 -> x0, waiting for transfers between devices: 72.9 us -> none  [on_device(): lax.psum_scatter(spread, 'slab', scatter_dimension=0, axis_index_groups=s...]
    all_to_all x1, waiting for transfers between devices: 23.7 us -> 0.01 us  [on_device(): got = lax.all_to_all(sent, both, 0, 0, axis_index_groups=near, tiled=True)]
    all_to_all x0 -> x1, starting transfers between devices: none -> 14 us  [on_device(): lax.all_to_all(notes, 'slab', 0, 0, axis_index_groups=slab_far, tiled=True)]
    ppermute x1, waiting for transfers between devices: 0.01 us -> 10.4 us  [on_device(): notes = lax.ppermute(notes, both, home_of)]
    all_to_all x1, blocking collectives: 31.8 us -> 40.8 us  [on_device(): lax.all_to_all(analysed.reshape(blocks, 8, 4, LANES), both, 0, 0, axis_in...]
    ppermute x1, waiting for transfers between devices: 0.01 us -> 6.48 us  [on_device(): high = lax.ppermute(got[:, 0], 'slab', fall)]
    pallas_call x1, Pallas kernels: 11.4 us -> 7.43 us  [on_device(): pl.pallas_call(functools.partial(pack_kernel, groups), out_shape=jax.Shap...]
    pallas_call x1 -> x0, Pallas kernels: 2.24 us -> none  [on_device(): pl.pallas_call(spread_kernel, out_shape=jax.ShapeDtypeStruct((rows, 10, 8...]
  transfers between devices with their start and end apart: 5 -> 5, of which waited for: 2 -> 2; matrix products, arithmetic and copies ran while one was open for 2% -> 2% of each run, Pallas kernels for 5% -> 0%
where the time goes in v3:
time: 144 us
  starting transfers between devices  53.1 us (37%)
  blocking collectives  40.8 us (28%)
  Pallas kernels  25.9 us (18%)
  waiting for transfers between devices  16.9 us (12%)
  local copies, waits for them, and re-layouts  6.46 us (4%)
    all_to_all x1, blocking collectives, on_device(): lax.all_to_all(analysed.reshape(blocks, 8, 4, LANES), both, 0, 0, axis_in...  40.8 us
    ppermute x1, starting transfers between devices, on_device(): notes = lax.ppermute(notes, both, home_of)  17.1 us
    pallas_call x1, Pallas kernels, on_device(): pl.pallas_call(functools.partial(analysis_kernel, groups, slabs), out_sha...  15.1 us
    all_to_all x1, starting transfers between devices, on_device(): lax.all_to_all(notes, 'slab', 0, 0, axis_index_groups=slab_far, tiled=True)  14 us
    all_to_all x1, starting transfers between devices, on_device(): got = lax.all_to_all(sent, both, 0, 0, axis_index_groups=near, tiled=True)  12.8 us
    ppermute x1, waiting for transfers between devices, on_device(): notes = lax.ppermute(notes, both, home_of)  10.4 us
    pallas_call x1, Pallas kernels, on_device(): pl.pallas_call(functools.partial(pack_kernel, groups), out_shape=jax.Shap...  7.43 us
    ppermute x1, waiting for transfers between devices, on_device(): high = lax.ppermute(got[:, 0], 'slab', fall)  6.48 us
  transfers between devices with their start and end apart: 5, of which 2 were waited for; matrix products, arithmetic and copies ran while one was open for 2% of the time, Pallas kernels for 0%

profile of v3, /device:TPU:57, one launch (start us, length us, event | category | flops | bytes accessed | tf_op | source)
XLA Modules:
  0.0 143.6 jit_solution(8306472016805706595)
XLA Ops:
  0.0 1.3 copy.21.diff_ref
  1.3 7.4 %pack.1 = bf16[96,10,4,128]{3,2,1,0:T(4,128)(2,1)} custom-call(s32[2]{0:T(128)} %prof_ref.1, f32[8,4]{1,0:T(8,128)} %copy.21.diff_ref, bf16[4,2,4,12288]{3,2,1,0:T(4,128)(2,1)} %x_ref.1, f32[2,2,12288]{2,1,0:T(2,128)} %ce_ref.1, f32[2,2,12288]{2,1,0:T(2,128)} %cn_ref.1), custom_call_target="tpu_custom_call" | custom-call | tf_op jit(solution)/shard_map/pack/pallas_call | solution.py:366
  8.8 12.8 %all-to-all-start = ((bf16[96,10,4,128]{3,2,1,0:T(4,128)(2,1)}), bf16[96,10,4,128]{3,2,1,0:T(4,128)(2,1)S(1)}, u32[]{:S(2)}, u32[]{:S(2)}) async-start(bf16[96,10,4,128]{3,2,1,0:T(4,128)(2,1)} %pack.1), calls=%async_computation | async-start | bytes 1966080 | tf_op jit(solution)/shard_map/all_to_all | solution.py:395
  21.6 0.1 copy.25
  21.9 0.1 stack_reshape.3
  22.0 0.6 copy-done.6
  22.7 0.1 reduce_sum.12
  22.9 0.6 copy-done.5
  23.5 0.1 sqrt_bitcast_fusion
  23.6 0.1 reshape.57
  23.8 17.1 %collective-permute-start.2 = (f32[8,2,8,128]{3,2,1,0:T(8,128)S(1)}, f32[8,2,8,128]{3,2,1,0:T(8,128)}, u32[]{:S(2)}, u32[]{:S(2)}) collective-permute-start(f32[8,2,8,128]{3,2,1,0:T(8,128)S(1)} %pad_maximum_fusion), channel_id=1, source_target_pairs={{0,0},{1,96},{2,192},{3,288},{4,384},{5,480},{6,576},{7,672},{8,12... | collective-permute-start | bytes 196616 | tf_op jit(solution)/shard_map/ppermute | solution.py:393
  40.8 10.4 %collective-permute-done.2 = f32[8,2,8,128]{3,2,1,0:T(8,128)} collective-permute-done((f32[8,2,8,128]{3,2,1,0:T(8,128)S(1)}, f32[8,2,8,128]{3,2,1,0:T(8,128)}, u32[]{:S(2)}, u32[]{:S(2)}) %collective-permute-start.2) | collective-permute-done | bytes 65568 | tf_op jit(solution)/shard_map/ppermute | solution.py:393
  51.3 14.0 %all-to-all-start.1 = ((f32[8,2,8,128]{3,2,1,0:T(8,128)}), f32[8,2,8,128]{3,2,1,0:T(8,128)S(1)}, u32[]{:S(2)}, u32[]{:S(2)}) async-start(f32[8,2,8,128]{3,2,1,0:T(8,128)} %collective-permute-done.2), calls=%async_computation.1 | async-start | bytes 131072 | tf_op jit(solution)/shard_map/all_to_all | solution.py:394
  65.3 0.2 copy.34
  65.5 0.3 fusion
  65.9 4.9 %collective-permute-start = (bf16[12,10,4,128]{3,2,1,0:T(4,128)(2,1)S(1)}, bf16[12,10,4,128]{3,2,1,0:T(4,128)(2,1)S(1)}, u32[]{:S(2)}, u32[]{:S(2)}) collective-permute-start(bf16[12,10,4,128]{3,2,1,0:T(4,128)(2,1)S(1)} %bitcast.25), channel_id=1, source_target_pairs={{0,96},{12,108},{24,120},{36,132},{48,144},{60,156},{72,168},{84,1... | collective-permute-start | bytes 368648 | tf_op jit(solution)/shard_map/ppermute | solution.py:397
  70.9 4.3 %collective-permute-start.1 = (bf16[12,10,4,128]{3,2,1,0:T(4,128)(2,1)S(1)}, bf16[12,10,4,128]{3,2,1,0:T(4,128)(2,1)S(1)}, u32[]{:S(2)}, u32[]{:S(2)}) collective-permute-start(bf16[12,10,4,128]{3,2,1,0:T(4,128)(2,1)S(1)} %bitcast.26), channel_id=1, source_target_pairs={{96,0},{108,12},{120,24},{132,36},{144,48},{156,60},{168,72},{180,... | collective-permute-start | bytes 368648 | tf_op jit(solution)/shard_map/ppermute | solution.py:398
  75.2 0.5 sqrt.7.ep_ref
  75.7 1.4 %copy.28.r_ref = bf16[12,8,10,4,128]{4,3,2,1,0:T(4,128)(2,1)} copy(bf16[12,8,10,4,128]{4,1,0,3,2:T(8,128)(2,1)S(1)} %bitcast.22) | data formatting | bytes 1966080 | tf_op jit(solution)/shard_map/reshape | solution.py:396
  77.2 6.5 %collective-permute-done.1.high_ref = bf16[12,10,4,128]{3,2,1,0:T(4,128)(2,1)S(1)} collective-permute-done((bf16[12,10,4,128]{3,2,1,0:T(4,128)(2,1)S(1)}, bf16[12,10,4,128]{3,2,1,0:T(4,128)(2,1)S(1)}, u32[]{:S(2)}, u32[]{:S(2)}) %collective-permute-start.1) | collective-permute-done | bytes 122912 | tf_op jit(solution)/shard_map/ppermute | solution.py:398
  83.7 0.7 copy-done.2
  84.3 15.1 %analysis.1 = bf16[12,8,8,4,128]{4,3,2,1,0:T(4,128)(2,1)} custom-call(f32[4]{0:T(128)} %sqrt.7.ep_ref, bf16[12,8,10,4,128]{4,3,2,1,0:T(4,128)(2,1)} %copy.28.r_ref, bf16[12,10,4,128]{3,2,1,0:T(4,128)(2,1)} %copy-done.1, bf16[12,10,4,128]{3,2,1,0:T(4,128)(2,1)} %copy-done.2, f32[8,2,8,128]{3,2,1,0:T(8,128)} %copy-done), custom_call_target="tpu_custom_call" | custom-call | tf_op jit(solution)/shard_map/analysis/pallas_call | solution.py:400
  99.5 40.8 %all_to_all.15.o_ref = bf16[96,8,4,128]{3,2,1,0:T(4,128)(2,1)} all-to-all(bf16[96,8,4,128]{3,2,1,0:T(4,128)(2,1)} %bitcast.23), channel_id=1, replica_groups={{0,12,24,36,48,60,72,84,1,13,25,37,49,61,73,85,2,14,26,38,50,62,74,86,3..., dimensions={0} | all-to-all | bytes 1572864 | tf_op jit(solution)/shard_map/all_to_all | solution.py:419
  140.3 3.3 %unpack.1 = bf16[4,2,4,12288]{3,2,1,0:T(4,128)(2,1)} custom-call(bf16[96,8,4,128]{3,2,1,0:T(4,128)(2,1)} %all_to_all.15.o_ref), custom_call_target="tpu_custom_call" | custom-call | tf_op jit(solution)/shard_map/unpack/pallas_call | solution.py:423
  (25 shorter events, 0.4 us)
Async XLA Ops:
  8.8 12.9 %copy-start.3 = (f32[128,4,16]{0,2,1:T(8,128)S(1)}, f32[128,4,16]{0,2,1:T(8,128)}, u32[]{:S(2)}) copy-start(f32[128,4,16]{0,2,1:T(8,128)} %param.15) | copy-start | bytes 98308
  8.8 42.5 %all-to-all-start = ((bf16[96,10,4,128]{3,2,1,0:T(4,128)(2,1)}), bf16[96,10,4,128]{3,2,1,0:T(4,128)(2,1)S(1)}, u32[]{:S(2)}, u32[]{:S(2)}) async-start(bf16[96,10,4,128]{3,2,1,0:T(4,128)(2,1)} %pack.1), calls=%async_computation | async-start | bytes 1966080 | tf_op jit(solution)/shard_map/all_to_all | solution.py:395
  21.8 0.8 copy-start.4
  22.0 0.7 copy-start.6
  22.8 0.7 copy-start.5
  23.8 27.5 %collective-permute-start.2 = (f32[8,2,8,128]{3,2,1,0:T(8,128)S(1)}, f32[8,2,8,128]{3,2,1,0:T(8,128)}, u32[]{:S(2)}, u32[]{:S(2)}) collective-permute-start(f32[8,2,8,128]{3,2,1,0:T(8,128)S(1)} %pad_maximum_fusion), channel_id=1, source_target_pairs={{0,0},{1,96},{2,192},{3,288},{4,384},{5,480},{6,576},{7,672},{8,12... | collective-permute-start | bytes 196616 | tf_op jit(solution)/shard_map/ppermute | solution.py:393
  51.3 25.9 %all-to-all-start.1 = ((f32[8,2,8,128]{3,2,1,0:T(8,128)}), f32[8,2,8,128]{3,2,1,0:T(8,128)S(1)}, u32[]{:S(2)}, u32[]{:S(2)}) async-start(f32[8,2,8,128]{3,2,1,0:T(8,128)} %collective-permute-done.2), calls=%async_computation.1 | async-start | bytes 131072 | tf_op jit(solution)/shard_map/all_to_all | solution.py:394
  65.9 11.3 %collective-permute-start = (bf16[12,10,4,128]{3,2,1,0:T(4,128)(2,1)S(1)}, bf16[12,10,4,128]{3,2,1,0:T(4,128)(2,1)S(1)}, u32[]{:S(2)}, u32[]{:S(2)}) collective-permute-start(bf16[12,10,4,128]{3,2,1,0:T(4,128)(2,1)S(1)} %bitcast.25), channel_id=1, source_target_pairs={{0,96},{12,108},{24,120},{36,132},{48,144},{60,156},{72,168},{84,1... | collective-permute-start | bytes 368648 | tf_op jit(solution)/shard_map/ppermute | solution.py:397
  70.8 4.3 %copy-start.7 = (f32[4]{0:T(128)S(1)}, f32[4]{0:T(128)}, u32[]{:S(2)}) copy-start(f32[4]{0:T(128)} %param.16) | copy-start | bytes 52
  70.9 12.8 %collective-permute-start.1 = (bf16[12,10,4,128]{3,2,1,0:T(4,128)(2,1)S(1)}, bf16[12,10,4,128]{3,2,1,0:T(4,128)(2,1)S(1)}, u32[]{:S(2)}, u32[]{:S(2)}) collective-permute-start(bf16[12,10,4,128]{3,2,1,0:T(4,128)(2,1)S(1)} %bitcast.26), channel_id=1, source_target_pairs={{96,0},{108,12},{120,24},{132,36},{144,48},{156,60},{168,72},{180,... | collective-permute-start | bytes 368648 | tf_op jit(solution)/shard_map/ppermute | solution.py:398
  77.2 6.5 %copy-start = (f32[8,2,8,128]{3,2,1,0:T(8,128)}, f32[8,2,8,128]{3,2,1,0:T(8,128)S(1)}, u32[]{:S(2)}) copy-start(f32[8,2,8,128]{3,2,1,0:T(8,128)S(1)} %all-to-all-done.1.rm_ref) | copy-start | bytes 196612
  77.2 6.5 %copy-start.1 = (bf16[12,10,4,128]{3,2,1,0:T(4,128)(2,1)}, bf16[12,10,4,128]{3,2,1,0:T(4,128)(2,1)S(1)}, u32[]{:S(2)}) copy-start(bf16[12,10,4,128]{3,2,1,0:T(4,128)(2,1)S(1)} %collective-permute-done.low_ref) | copy-start | bytes 368644
  83.7 0.7 copy-start.2

commit v4 on v3

--- a/solution.py
+++ b/solution.py
@@ -123,9 +123,11 @@
 
 
 def analysis_kernel(
-    groups, slabs, ep_ref, r_ref, low_ref, high_ref, rm_ref,
-    y_ref, x0, hx, hs, x1, bg, dev, wts, rc_ref
-):
+    groups, slabs, ep_ref, r_ref, low_ref, high_ref, *refs):
+    rounds = refs[:8]
+    y_ref, x0, hx, hs, x1, bg, dev, wts, rc_ref, rm_ref = refs[8:]
+    for k in range(8):
+        rm_ref[lax.rem(lax.axis_index("slab") // ROWS + 8 - k, 8)] = rounds[k][...]
     members = 4 * groups
     slab = lax.axis_index("slab")
     row = slab // ROWS
@@ -329,17 +331,21 @@
 
 
 def unpack_kernel(o_ref, out_ref):
+    sub8 = lax.rem(lax.broadcasted_iota(jnp.int32, (8, LANES), 0), 4)
+
     def one(b, carry):
         at = pl.ds(pl.multiple_of(b * LANES, LANES), LANES)
-        for r in range(2):
-            x = [o_ref[b, r * 4 + v].astype(F32) for v in range(4)]
-            for m in range(4):
-                out_ref[m, r, :, at] = jnp.concatenate(
-                    [x[v][m : m + 1] for v in range(4)], axis=0
-                ).astype(BF16)
-        return carry
-
-    lax.fori_loop(0, o_ref.shape[0], one, 0)
+        x = [jnp.concatenate([o_ref[b, v].astype(F32), o_ref[b, 4 + v].astype(F32)], axis=0) for v in range(4)]
+        for m in range(4):
+            tile = x[m]
+            for v in range(4):
+                if m != v:
+                    tile = jnp.where(sub8 == v, pltpu.roll(x[v], (v - m) % 8, 0), tile)
+            out_ref[m, 0, :, at] = tile[0:4].astype(BF16)
+            out_ref[m, 1, :, at] = tile[4:8].astype(BF16)
+        return carry
+
+    lax.fori_loop(0, o_ref.shape[0], one, 0, unroll=4)
 
 
 def on_device(
@@ -383,16 +389,20 @@
 
     both = ("slab", "grp")
     near = [[(r * ROWS + i) * groups + g for g in range(groups) for i in range(ROWS)] for r in range(rows)]
-    slab_far = [[r * ROWS + i for r in range(rows)] for i in range(ROWS)]
     rise = [(s, s + ROWS) for s in range(slabs - ROWS)]
     fall = [(s + ROWS, s) for s in range(slabs - ROWS)]
 
-    home_of = [
-        (f, ((f % 8) * ROWS + (f // 8) % ROWS) * groups + f // (8 * ROWS)) for f in range(slabs * groups)
-    ]
-    notes = lax.ppermute(notes, both, home_of)
-    got_m = lax.all_to_all(notes, "slab", 0, 0, axis_index_groups=slab_far, tiled=True)
+    flat = lax.axis_index("slab") * groups + lax.axis_index("grp")
+    turned = lax.dynamic_slice_in_dim(jnp.concatenate([notes, notes]), lax.rem(flat, 8), 8)
+    rounds = []
+    for k in range(8):
+        route = [
+            (f, (((f + k) % 8) * ROWS + (f // 8) % ROWS) * groups + f // (8 * ROWS))
+            for f in range(slabs * groups)
+        ]
+        rounds.append(lax.ppermute(turned[k], both, route))
     got = lax.all_to_all(sent, both, 0, 0, axis_index_groups=near, tiled=True)
+    got, *rounds = lax.optimization_barrier((got, *rounds))
     got = got.reshape(groups, ROWS, 10, 4, LANES)
     low = lax.ppermute(got[:, ROWS - 1], "slab", rise)
     high = lax.ppermute(got[:, 0], "slab", fall)
@@ -400,7 +410,7 @@
     analysed = pl.pallas_call(
         functools.partial(analysis_kernel, groups, slabs),
         out_shape=jax.ShapeDtypeStruct((groups, ROWS, 8, 4, LANES), BF16),
-        in_specs=[smem] + [vmem] * 4,
+        in_specs=[smem] + [vmem] * 11,
         out_specs=vmem,
         scratch_shapes=[
             pltpu.VMEM((80, members, LANES), F32),
@@ -411,10 +421,11 @@
             pltpu.VMEM((8, PAD, 8 * LANES), BF16),
             pltpu.VMEM((2 * members, 8 * PAD), BF16),
             pltpu.VMEM((10, 24, LANES), F32),
+            pltpu.VMEM((8, 2, 8, LANES), F32),
         ],
         compiler_params=params,
         name="analysis",
-    )(jnp.sqrt(error_precision), got, low, high, got_m)
+    )(jnp.sqrt(error_precision), got, low, high, *rounds)
 
     home = lax.all_to_all(
         analysed.reshape(blocks, 8, 4, LANES), both, 0, 0, axis_index_groups=near, tiled=True

time: 144 us -> 168 us (1.17); the launches traced: 144 us -> 166 us
  starting transfers between devices: 53.1 us -> 81.9 us
  waiting for transfers between devices: 16.9 us -> 11.8 us
    ppermute x1 -> x8, starting transfers between devices: 17.1 us -> 59.8 us  [on_device(): rounds.append(lax.ppermute(turned[k], both, route))]
    all_to_all x1 -> x0, starting transfers between devices: 14 us -> none  [on_device(): lax.all_to_all(notes, 'slab', 0, 0, axis_index_groups=slab_far, tiled=True)]
    ppermute x1 -> x8, waiting for transfers between devices: 10.4 us -> 7.07 us  [on_device(): rounds.append(lax.ppermute(turned[k], both, route))]
    ppermute x1, starting transfers between devices: 4.3 us -> 7.27 us  [on_device(): high = lax.ppermute(got[:, 0], 'slab', fall)]
    ppermute x1, starting transfers between devices: 4.89 us -> 1.92 us  [on_device(): low = lax.ppermute(got[:, ROWS - 1], 'slab', rise)]
    ppermute x1, waiting for transfers between devices: 6.48 us -> 4.71 us  [on_device(): high = lax.ppermute(got[:, 0], 'slab', fall)]
    unnamed x20 -> x34, local copies, waits for them, and re-layouts: 3.6 us -> 3.96 us
  transfers between devices with their start and end apart: 5 -> 11, of which waited for: 2 -> 2; matrix products, arithmetic and copies ran while one was open for 2% -> 2% of each run, Pallas kernels for 0% -> 0%
where the time goes in v4:
time: 168 us; the launch traced here: 166 us
  starting transfers between devices  81.9 us (49%)
  blocking collectives  39.2 us (23%)
  Pallas kernels  25.5 us (15%)
  waiting for transfers between devices  11.8 us (7%)
  local copies, waits for them, and re-layouts  6.87 us (4%)
    ppermute x8, starting transfers between devices, on_device(): rounds.append(lax.ppermute(turned[k], both, route))  59.8 us
    all_to_all x1, blocking collectives, on_device(): lax.all_to_all(analysed.reshape(blocks, 8, 4, LANES), both, 0, 0, axis_in...  39.2 us
    pallas_call x1, Pallas kernels, on_device(): pl.pallas_call(functools.partial(analysis_kernel, groups, slabs), out_sha...  15.2 us
    all_to_all x1, starting transfers between devices, on_device(): got = lax.all_to_all(sent, both, 0, 0, axis_index_groups=near, tiled=True)  12.8 us
    pallas_call x1, Pallas kernels, on_device(): pl.pallas_call(functools.partial(pack_kernel, groups), out_shape=jax.Shap...  7.47 us
    ppermute x1, starting transfers between devices, on_device(): high = lax.ppermute(got[:, 0], 'slab', fall)  7.27 us
    ppermute x8, waiting for transfers between devices, on_device(): rounds.append(lax.ppermute(turned[k], both, route))  7.07 us
    ppermute x1, waiting for transfers between devices, on_device(): high = lax.ppermute(got[:, 0], 'slab', fall)  4.71 us
  transfers between devices with their start and end apart: 11, of which 2 were waited for; matrix products, arithmetic and copies ran while one was open for 2% of the time, Pallas kernels for 0%

profile of v4, /device:TPU:57, one launch (start us, length us, event | category | flops | bytes accessed | tf_op | source)
XLA Modules:
  0.0 165.8 jit_solution(17350525918825784119)
XLA Ops:
  0.0 1.3 copy.21.diff_ref
  1.3 7.5 %pack.1 = bf16[96,10,4,128]{3,2,1,0:T(4,128)(2,1)} custom-call(s32[2]{0:T(128)} %prof_ref.1, f32[8,4]{1,0:T(8,128)} %copy.21.diff_ref, bf16[4,2,4,12288]{3,2,1,0:T(4,128)(2,1)} %x_ref.1, f32[2,2,12288]{2,1,0:T(2,128)} %ce_ref.1, f32[2,2,12288]{2,1,0:T(2,128)} %cn_ref.1), custom_call_target="tpu_custom_call" | custom-call | tf_op jit(solution)/shard_map/pack/pallas_call | solution.py:372
  8.8 12.8 %all-to-all-start = ((bf16[96,10,4,128]{3,2,1,0:T(4,128)(2,1)}), bf16[96,10,4,128]{3,2,1,0:T(4,128)(2,1)S(1)}, u32[]{:S(2)}, u32[]{:S(2)}) async-start(bf16[96,10,4,128]{3,2,1,0:T(4,128)(2,1)} %pack.1), calls=%async_computation | async-start | bytes 1966080 | tf_op jit(solution)/shard_map/all_to_all | solution.py:404
  22.1 0.6 copy-done.13
  22.9 0.6 copy-done.12
  23.9 17.1 %collective-permute-start = (f32[2,8,128]{2,1,0:T(8,128)S(1)}, f32[2,8,128]{2,1,0:T(8,128)S(1)}, u32[]{:S(2)}, u32[]{:S(2)}) collective-permute-start(f32[2,8,128]{2,1,0:T(8,128)S(1)} %get-tuple-element.32), channel_id=1, source_target_pairs={{0,0},{1,96},{2,192},{3,288},{4,384},{5,480},{6,576},{7,672},{8,12... | collective-permute-start | bytes 24584 | tf_op jit(solution)/shard_map/ppermute | solution.py:403
  41.0 2.8 %collective-permute-start.1 = (f32[2,8,128]{2,1,0:T(8,128)S(1)}, f32[2,8,128]{2,1,0:T(8,128)S(1)}, u32[]{:S(2)}, u32[]{:S(2)}) collective-permute-start(f32[2,8,128]{2,1,0:T(8,128)S(1)} %get-tuple-element.31), channel_id=1, source_target_pairs={{0,96},{1,192},{2,288},{3,384},{4,480},{5,576},{6,672},{7,0},{8,10... | collective-permute-start | bytes 24584 | tf_op jit(solution)/shard_map/ppermute | solution.py:403
  43.8 12.8 %collective-permute-start.2 = (f32[2,8,128]{2,1,0:T(8,128)S(1)}, f32[2,8,128]{2,1,0:T(8,128)S(1)}, u32[]{:S(2)}, u32[]{:S(2)}) collective-permute-start(f32[2,8,128]{2,1,0:T(8,128)S(1)} %get-tuple-element.30), channel_id=1, source_target_pairs={{0,192},{1,288},{2,384},{3,480},{4,576},{5,672},{6,0},{7,96},{8,20... | collective-permute-start | bytes 24584 | tf_op jit(solution)/shard_map/ppermute | solution.py:403
  56.6 1.9 %collective-permute-start.3 = (f32[2,8,128]{2,1,0:T(8,128)S(1)}, f32[2,8,128]{2,1,0:T(8,128)S(1)}, u32[]{:S(2)}, u32[]{:S(2)}) collective-permute-start(f32[2,8,128]{2,1,0:T(8,128)S(1)} %get-tuple-element.29), channel_id=1, source_target_pairs={{0,288},{1,384},{2,480},{3,576},{4,672},{5,0},{6,96},{7,192},{8,30... | collective-permute-start | bytes 24584 | tf_op jit(solution)/shard_map/ppermute | solution.py:403
  58.5 4.5 %collective-permute-start.4 = (f32[2,8,128]{2,1,0:T(8,128)S(1)}, f32[2,8,128]{2,1,0:T(8,128)S(1)}, u32[]{:S(2)}, u32[]{:S(2)}) collective-permute-start(f32[2,8,128]{2,1,0:T(8,128)S(1)} %get-tuple-element.28), channel_id=1, source_target_pairs={{0,384},{1,480},{2,576},{3,672},{4,0},{5,96},{6,192},{7,288},{8,39... | collective-permute-start | bytes 24584 | tf_op jit(solution)/shard_map/ppermute | solution.py:403
  63.1 6.4 %collective-permute-start.5 = (f32[2,8,128]{2,1,0:T(8,128)S(1)}, f32[2,8,128]{2,1,0:T(8,128)S(1)}, u32[]{:S(2)}, u32[]{:S(2)}) collective-permute-start(f32[2,8,128]{2,1,0:T(8,128)S(1)} %get-tuple-element.27), channel_id=1, source_target_pairs={{0,480},{1,576},{2,672},{3,0},{4,96},{5,192},{6,288},{7,384},{8,49... | collective-permute-start | bytes 24584 | tf_op jit(solution)/shard_map/ppermute | solution.py:403
  69.5 10.4 %collective-permute-start.6 = (f32[2,8,128]{2,1,0:T(8,128)S(1)}, f32[2,8,128]{2,1,0:T(8,128)S(1)}, u32[]{:S(2)}, u32[]{:S(2)}) collective-permute-start(f32[2,8,128]{2,1,0:T(8,128)S(1)} %get-tuple-element.26), channel_id=1, source_target_pairs={{0,576},{1,672},{2,0},{3,96},{4,192},{5,288},{6,384},{7,480},{8,58... | collective-permute-start | bytes 24584 | tf_op jit(solution)/shard_map/ppermute | solution.py:403
  79.9 3.8 %collective-permute-start.7 = (f32[2,8,128]{2,1,0:T(8,128)S(1)}, f32[2,8,128]{2,1,0:T(8,128)S(1)}, u32[]{:S(2)}, u32[]{:S(2)}) collective-permute-start(f32[2,8,128]{2,1,0:T(8,128)S(1)} %get-tuple-element.25), channel_id=1, source_target_pairs={{0,672},{1,0},{2,96},{3,192},{4,288},{5,384},{6,480},{7,576},{8,68... | collective-permute-start | bytes 24584 | tf_op jit(solution)/shard_map/ppermute | solution.py:403
  83.9 7.0 %collective-permute-done.7.refs_7_ = f32[2,8,128]{2,1,0:T(8,128)S(1)} collective-permute-done((f32[2,8,128]{2,1,0:T(8,128)S(1)}, f32[2,8,128]{2,1,0:T(8,128)S(1)}, u32[]{:S(2)}, u32[]{:S(2)}) %collective-permute-start.7) | collective-permute-done | bytes 8224 | tf_op jit(solution)/shard_map/ppermute | solution.py:403
  91.2 0.3 copy-done.10
  91.9 1.9 %collective-permute-start.8 = (bf16[12,10,4,128]{3,2,1,0:T(4,128)(2,1)S(1)}, bf16[12,10,4,128]{3,2,1,0:T(4,128)(2,1)S(1)}, u32[]{:S(2)}, u32[]{:S(2)}) collective-permute-start(bf16[12,10,4,128]{3,2,1,0:T(4,128)(2,1)S(1)} %bitcast.41), channel_id=1, source_target_pairs={{0,96},{12,108},{24,120},{36,132},{48,144},{60,156},{72,168},{84,1... | collective-permute-start | bytes 368648 | tf_op jit(solution)/shard_map/ppermute | solution.py:407
  93.9 7.3 %collective-permute-start.9 = (bf16[12,10,4,128]{3,2,1,0:T(4,128)(2,1)S(1)}, bf16[12,10,4,128]{3,2,1,0:T(4,128)(2,1)S(1)}, u32[]{:S(2)}, u32[]{:S(2)}) collective-permute-start(bf16[12,10,4,128]{3,2,1,0:T(4,128)(2,1)S(1)} %bitcast.42), channel_id=1, source_target_pairs={{96,0},{108,12},{120,24},{132,36},{144,48},{156,60},{168,72},{180,... | collective-permute-start | bytes 368648 | tf_op jit(solution)/shard_map/ppermute | solution.py:408
  101.2 0.5 sqrt.7.ep_ref
  101.8 1.5 copy.28.r_ref
  103.3 4.7 %collective-permute-done.9.high_ref = bf16[12,10,4,128]{3,2,1,0:T(4,128)(2,1)S(1)} collective-permute-done((bf16[12,10,4,128]{3,2,1,0:T(4,128)(2,1)S(1)}, bf16[12,10,4,128]{3,2,1,0:T(4,128)(2,1)S(1)}, u32[]{:S(2)}, u32[]{:S(2)}) %collective-permute-start.9) | collective-permute-done | bytes 122912 | tf_op jit(solution)/shard_map/ppermute | solution.py:408
  108.0 0.6 copy-done.1
  108.6 15.2 %analysis.1 = bf16[12,8,8,4,128]{4,3,2,1,0:T(4,128)(2,1)} custom-call(f32[4]{0:T(128)} %sqrt.7.ep_ref, bf16[12,8,10,4,128]{4,3,2,1,0:T(4,128)(2,1)} %copy.28.r_ref, bf16[12,10,4,128]{3,2,1,0:T(4,128)(2,1)} %copy-done, bf16[12,10,4,128]{3,2,1,0:T(4,128)(2,1)} %copy-done.1, f32[2,8,128]{2,1,0:T(8,128)} %copy-done.3, f32[2,8,128]{2,1,0:T(8,128)} %copy-done.4, ...), custom_call_target="tpu_custom_call" | custom-call | tf_op jit(solution)/shard_map/analysis/pallas_call | solution.py:410
  123.8 39.2 %all_to_all.10.o_ref = bf16[96,8,4,128]{3,2,1,0:T(4,128)(2,1)} all-to-all(bf16[96,8,4,128]{3,2,1,0:T(4,128)(2,1)} %bitcast.39), channel_id=1, replica_groups={{0,12,24,36,48,60,72,84,1,13,25,37,49,61,73,85,2,14,26,38,50,62,74,86,3..., dimensions={0} | all-to-all | bytes 1572864 | tf_op jit(solution)/shard_map/all_to_all | solution.py:430
  163.0 2.9 %unpack.1 = bf16[4,2,4,12288]{3,2,1,0:T(4,128)(2,1)} custom-call(bf16[96,8,4,128]{3,2,1,0:T(4,128)(2,1)} %all_to_all.10.o_ref), custom_call_target="tpu_custom_call" | custom-call | tf_op jit(solution)/shard_map/unpack/pallas_call | solution.py:434
  (52 shorter events, 1.5 us)
Async XLA Ops:
  8.8 12.9 %copy-start.2 = (f32[128,4,16]{0,2,1:T(8,128)S(1)}, f32[128,4,16]{0,2,1:T(8,128)}, u32[]{:S(2)}) copy-start(f32[128,4,16]{0,2,1:T(8,128)} %param.15) | copy-start | bytes 98308
  8.8 82.1 %all-to-all-start = ((bf16[96,10,4,128]{3,2,1,0:T(4,128)(2,1)}), bf16[96,10,4,128]{3,2,1,0:T(4,128)(2,1)S(1)}, u32[]{:S(2)}, u32[]{:S(2)}) async-start(bf16[96,10,4,128]{3,2,1,0:T(4,128)(2,1)} %pack.1), calls=%async_computation | async-start | bytes 1966080 | tf_op jit(solution)/shard_map/all_to_all | solution.py:404
  21.9 0.8 copy-start.11
  22.1 0.7 copy-start.13
  22.9 0.7 copy-start.12
  23.9 39.2 %collective-permute-start = (f32[2,8,128]{2,1,0:T(8,128)S(1)}, f32[2,8,128]{2,1,0:T(8,128)S(1)}, u32[]{:S(2)}, u32[]{:S(2)}) collective-permute-start(f32[2,8,128]{2,1,0:T(8,128)S(1)} %get-tuple-element.32), channel_id=1, source_target_pairs={{0,0},{1,96},{2,192},{3,288},{4,384},{5,480},{6,576},{7,672},{8,12... | collective-permute-start | bytes 24584 | tf_op jit(solution)/shard_map/ppermute | solution.py:403
  41.0 28.5 %collective-permute-start.1 = (f32[2,8,128]{2,1,0:T(8,128)S(1)}, f32[2,8,128]{2,1,0:T(8,128)S(1)}, u32[]{:S(2)}, u32[]{:S(2)}) collective-permute-start(f32[2,8,128]{2,1,0:T(8,128)S(1)} %get-tuple-element.31), channel_id=1, source_target_pairs={{0,96},{1,192},{2,288},{3,384},{4,480},{5,576},{6,672},{7,0},{8,10... | collective-permute-start | bytes 24584 | tf_op jit(solution)/shard_map/ppermute | solution.py:403
  43.8 36.2 %collective-permute-start.2 = (f32[2,8,128]{2,1,0:T(8,128)S(1)}, f32[2,8,128]{2,1,0:T(8,128)S(1)}, u32[]{:S(2)}, u32[]{:S(2)}) collective-permute-start(f32[2,8,128]{2,1,0:T(8,128)S(1)} %get-tuple-element.30), channel_id=1, source_target_pairs={{0,192},{1,288},{2,384},{3,480},{4,576},{5,672},{6,0},{7,96},{8,20... | collective-permute-start | bytes 24584 | tf_op jit(solution)/shard_map/ppermute | solution.py:403
  56.6 27.2 %collective-permute-start.3 = (f32[2,8,128]{2,1,0:T(8,128)S(1)}, f32[2,8,128]{2,1,0:T(8,128)S(1)}, u32[]{:S(2)}, u32[]{:S(2)}) collective-permute-start(f32[2,8,128]{2,1,0:T(8,128)S(1)} %get-tuple-element.29), channel_id=1, source_target_pairs={{0,288},{1,384},{2,480},{3,576},{4,672},{5,0},{6,96},{7,192},{8,30... | collective-permute-start | bytes 24584 | tf_op jit(solution)/shard_map/ppermute | solution.py:403
  58.5 25.3 %collective-permute-start.4 = (f32[2,8,128]{2,1,0:T(8,128)S(1)}, f32[2,8,128]{2,1,0:T(8,128)S(1)}, u32[]{:S(2)}, u32[]{:S(2)}) collective-permute-start(f32[2,8,128]{2,1,0:T(8,128)S(1)} %get-tuple-element.28), channel_id=1, source_target_pairs={{0,384},{1,480},{2,576},{3,672},{4,0},{5,96},{6,192},{7,288},{8,39... | collective-permute-start | bytes 24584 | tf_op jit(solution)/shard_map/ppermute | solution.py:403
  63.0 28.1 %copy-start.3 = (f32[2,8,128]{2,1,0:T(8,128)}, f32[2,8,128]{2,1,0:T(8,128)S(1)}, u32[]{:S(2)}) copy-start(f32[2,8,128]{2,1,0:T(8,128)S(1)} %collective-permute-done.refs_0_) | copy-start | bytes 24580
  63.1 20.8 %collective-permute-start.5 = (f32[2,8,128]{2,1,0:T(8,128)S(1)}, f32[2,8,128]{2,1,0:T(8,128)S(1)}, u32[]{:S(2)}, u32[]{:S(2)}) collective-permute-start(f32[2,8,128]{2,1,0:T(8,128)S(1)} %get-tuple-element.27), channel_id=1, source_target_pairs={{0,480},{1,576},{2,672},{3,0},{4,96},{5,192},{6,288},{7,384},{8,49... | collective-permute-start | bytes 24584 | tf_op jit(solution)/shard_map/ppermute | solution.py:403
  69.5 21.7 %copy-start.4 = (f32[2,8,128]{2,1,0:T(8,128)}, f32[2,8,128]{2,1,0:T(8,128)S(1)}, u32[]{:S(2)}) copy-start(f32[2,8,128]{2,1,0:T(8,128)S(1)} %collective-permute-done.1.refs_1_) | copy-start | bytes 24580
  69.5 14.4 %collective-permute-start.6 = (f32[2,8,128]{2,1,0:T(8,128)S(1)}, f32[2,8,128]{2,1,0:T(8,128)S(1)}, u32[]{:S(2)}, u32[]{:S(2)}) collective-permute-start(f32[2,8,128]{2,1,0:T(8,128)S(1)} %get-tuple-element.26), channel_id=1, source_target_pairs={{0,576},{1,672},{2,0},{3,96},{4,192},{5,288},{6,384},{7,480},{8,58... | collective-permute-start | bytes 24584 | tf_op jit(solution)/shard_map/ppermute | solution.py:403
  79.9 11.2 %copy-start.5 = (f32[2,8,128]{2,1,0:T(8,128)}, f32[2,8,128]{2,1,0:T(8,128)S(1)}, u32[]{:S(2)}) copy-start(f32[2,8,128]{2,1,0:T(8,128)S(1)} %collective-permute-done.2.refs_2_) | copy-start | bytes 24580
  79.9 11.0 %collective-permute-start.7 = (f32[2,8,128]{2,1,0:T(8,128)S(1)}, f32[2,8,128]{2,1,0:T(8,128)S(1)}, u32[]{:S(2)}, u32[]{:S(2)}) collective-permute-start(f32[2,8,128]{2,1,0:T(8,128)S(1)} %get-tuple-element.25), channel_id=1, source_target_pairs={{0,672},{1,0},{2,96},{3,192},{4,288},{5,384},{6,480},{7,576},{8,68... | collective-permute-start | bytes 24584 | tf_op jit(solution)/shard_map/ppermute | solution.py:403
  83.8 7.3 %copy-start.6 = (f32[2,8,128]{2,1,0:T(8,128)}, f32[2,8,128]{2,1,0:T(8,128)S(1)}, u32[]{:S(2)}) copy-start(f32[2,8,128]{2,1,0:T(8,128)S(1)} %collective-permute-done.3.refs_3_) | copy-start | bytes 24580
  83.8 7.3 %copy-start.7 = (f32[2,8,128]{2,1,0:T(8,128)}, f32[2,8,128]{2,1,0:T(8,128)S(1)}, u32[]{:S(2)}) copy-start(f32[2,8,128]{2,1,0:T(8,128)S(1)} %collective-permute-done.4.refs_4_) | copy-start | bytes 24580
  83.9 7.3 %copy-start.8 = (f32[2,8,128]{2,1,0:T(8,128)}, f32[2,8,128]{2,1,0:T(8,128)S(1)}, u32[]{:S(2)}) copy-start(f32[2,8,128]{2,1,0:T(8,128)S(1)} %collective-permute-done.5.refs_5_) | copy-start | bytes 24580
  83.9 7.3 %copy-start.9 = (f32[2,8,128]{2,1,0:T(8,128)}, f32[2,8,128]{2,1,0:T(8,128)S(1)}, u32[]{:S(2)}) copy-start(f32[2,8,128]{2,1,0:T(8,128)S(1)} %collective-permute-done.6.refs_6_) | copy-start | bytes 24580
  91.9 11.3 %collective-permute-start.8 = (bf16[12,10,4,128]{3,2,1,0:T(4,128)(2,1)S(1)}, bf16[12,10,4,128]{3,2,1,0:T(4,128)(2,1)S(1)}, u32[]{:S(2)}, u32[]{:S(2)}) collective-permute-start(bf16[12,10,4,128]{3,2,1,0:T(4,128)(2,1)S(1)} %bitcast.41), channel_id=1, source_target_pairs={{0,96},{12,108},{24,120},{36,132},{48,144},{60,156},{72,168},{84,1... | collective-permute-start | bytes 368648 | tf_op jit(solution)/shard_map/ppermute | solution.py:407
  93.9 7.3 %copy-start.14 = (f32[4]{0:T(128)S(1)}, f32[4]{0:T(128)}, u32[]{:S(2)}) copy-start(f32[4]{0:T(128)} %param.16) | copy-start | bytes 52
  93.9 14.0 %collective-permute-start.9 = (bf16[12,10,4,128]{3,2,1,0:T(4,128)(2,1)S(1)}, bf16[12,10,4,128]{3,2,1,0:T(4,128)(2,1)S(1)}, u32[]{:S(2)}, u32[]{:S(2)}) collective-permute-start(bf16[12,10,4,128]{3,2,1,0:T(4,128)(2,1)S(1)} %bitcast.42), channel_id=1, source_target_pairs={{96,0},{108,12},{120,24},{132,36},{144,48},{156,60},{168,72},{180,... | collective-permute-start | bytes 368648 | tf_op jit(solution)/shard_map/ppermute | solution.py:408
  103.3 4.7 %copy-start = (bf16[12,10,4,128]{3,2,1,0:T(4,128)(2,1)}, bf16[12,10,4,128]{3,2,1,0:T(4,128)(2,1)S(1)}, u32[]{:S(2)}) copy-start(bf16[12,10,4,128]{3,2,1,0:T(4,128)(2,1)S(1)} %collective-permute-done.8.low_ref) | copy-start | bytes 368644
  (2 other events, 1.2 us)

commit v5 on v3

--- a/solution.py
+++ b/solution.py
@@ -329,17 +329,21 @@
 
 
 def unpack_kernel(o_ref, out_ref):
+    sub8 = lax.rem(lax.broadcasted_iota(jnp.int32, (8, LANES), 0), 4)
+
     def one(b, carry):
         at = pl.ds(pl.multiple_of(b * LANES, LANES), LANES)
-        for r in range(2):
-            x = [o_ref[b, r * 4 + v].astype(F32) for v in range(4)]
-            for m in range(4):
-                out_ref[m, r, :, at] = jnp.concatenate(
-                    [x[v][m : m + 1] for v in range(4)], axis=0
-                ).astype(BF16)
-        return carry
-
-    lax.fori_loop(0, o_ref.shape[0], one, 0)
+        x = [jnp.concatenate([o_ref[b, v].astype(F32), o_ref[b, 4 + v].astype(F32)], axis=0) for v in range(4)]
+        for m in range(4):
+            tile = x[m]
+            for v in range(4):
+                if m != v:
+                    tile = jnp.where(sub8 == v, pltpu.roll(x[v], (v - m) % 8, 0), tile)
+            out_ref[m, 0, :, at] = tile[0:4].astype(BF16)
+            out_ref[m, 1, :, at] = tile[4:8].astype(BF16)
+        return carry
+
+    lax.fori_loop(0, o_ref.shape[0], one, 0, unroll=4)
 
 
 def on_device(
@@ -391,11 +395,12 @@
         (f, ((f % 8) * ROWS + (f // 8) % ROWS) * groups + f // (8 * ROWS)) for f in range(slabs * groups)
     ]
     notes = lax.ppermute(notes, both, home_of)
-    got_m = lax.all_to_all(notes, "slab", 0, 0, axis_index_groups=slab_far, tiled=True)
     got = lax.all_to_all(sent, both, 0, 0, axis_index_groups=near, tiled=True)
     got = got.reshape(groups, ROWS, 10, 4, LANES)
-    low = lax.ppermute(got[:, ROWS - 1], "slab", rise)
-    high = lax.ppermute(got[:, 0], "slab", fall)
+    last, first, notes = lax.optimization_barrier((got[:, ROWS - 1], got[:, 0], notes))
+    low = lax.ppermute(last, "slab", rise)
+    high = lax.ppermute(first, "slab", fall)
+    got_m = lax.all_to_all(notes, "slab", 0, 0, axis_index_groups=slab_far, tiled=True)
 
     analysed = pl.pallas_call(
         functools.partial(analysis_kernel, groups, slabs),

time: 144 us -> 144 us (level)
    ppermute x1, waiting for transfers between devices: 10.4 us -> 4.6 us  [on_device(): notes = lax.ppermute(notes, both, home_of)]
    all_to_all x1, waiting for transfers between devices: 0.01 us -> 5.19 us  [on_device(): got = lax.all_to_all(sent, both, 0, 0, axis_index_groups=near, tiled=True)]
    unnamed x20 -> x18, local copies, waits for them, and re-layouts: 3.6 us -> 4.1 us
  transfers between devices with their start and end apart: 5 -> 5, of which waited for: 2 -> 3; matrix products, arithmetic and copies ran while one was open for 2% -> 2% of each run, Pallas kernels for 0% -> 0%
where the time goes in v5:
time: 144 us
  starting transfers between devices  53.8 us (37%)
  blocking collectives  40.8 us (28%)
  Pallas kernels  25.4 us (18%)
  waiting for transfers between devices  16.3 us (11%)
  local copies, waits for them, and re-layouts  7.08 us (5%)
    all_to_all x1, blocking collectives, on_device(): lax.all_to_all(analysed.reshape(blocks, 8, 4, LANES), both, 0, 0, axis_in...  40.8 us
    ppermute x1, starting transfers between devices, on_device(): notes = lax.ppermute(notes, both, home_of)  17.1 us
    pallas_call x1, Pallas kernels, on_device(): pl.pallas_call(functools.partial(analysis_kernel, groups, slabs), out_sha...  15.1 us
    all_to_all x1, starting transfers between devices, on_device(): lax.all_to_all(notes, 'slab', 0, 0, axis_index_groups=slab_far, tiled=True)  14.7 us
    all_to_all x1, starting transfers between devices, on_device(): got = lax.all_to_all(sent, both, 0, 0, axis_index_groups=near, tiled=True)  12.8 us
    pallas_call x1, Pallas kernels, on_device(): pl.pallas_call(functools.partial(pack_kernel, groups), out_shape=jax.Shap...  7.44 us
    ppermute x1, waiting for transfers between devices, on_device(): high = lax.ppermute(first, 'slab', fall)  6.5 us
    all_to_all x1, waiting for transfers between devices, on_device(): got = lax.all_to_all(sent, both, 0, 0, axis_index_groups=near, tiled=True)  5.19 us
  transfers between devices with their start and end apart: 5, of which 3 were waited for; matrix products, arithmetic and copies ran while one was open for 2% of the time, Pallas kernels for 0%

profile of v5, /device:TPU:57, one launch (start us, length us, event | category | flops | bytes accessed | tf_op | source)
XLA Modules:
  0.0 143.8 jit_solution(4090209293209024271)
XLA Ops:
  0.0 1.3 copy.21.diff_ref
  1.3 7.4 %pack.1 = bf16[96,10,4,128]{3,2,1,0:T(4,128)(2,1)} custom-call(s32[2]{0:T(128)} %prof_ref.1, f32[8,4]{1,0:T(8,128)} %copy.21.diff_ref, bf16[4,2,4,12288]{3,2,1,0:T(4,128)(2,1)} %x_ref.1, f32[2,2,12288]{2,1,0:T(2,128)} %ce_ref.1, f32[2,2,12288]{2,1,0:T(2,128)} %cn_ref.1), custom_call_target="tpu_custom_call" | custom-call | tf_op jit(solution)/shard_map/pack/pallas_call | solution.py:370
  8.8 12.8 %all-to-all-start = ((bf16[96,10,4,128]{3,2,1,0:T(4,128)(2,1)}), bf16[96,10,4,128]{3,2,1,0:T(4,128)(2,1)S(1)}, u32[]{:S(2)}, u32[]{:S(2)}) async-start(bf16[96,10,4,128]{3,2,1,0:T(4,128)(2,1)} %pack.1), calls=%async_computation | async-start | bytes 1966080 | tf_op jit(solution)/shard_map/all_to_all | solution.py:398
  21.6 0.1 copy.25
  21.9 0.1 stack_reshape.3
  22.0 0.6 copy-done.6
  22.9 0.6 copy-done.5
  23.8 17.1 %collective-permute-start = (f32[8,2,8,128]{3,2,1,0:T(8,128)S(1)}, f32[8,2,8,128]{3,2,1,0:T(8,128)}, u32[]{:S(2)}, u32[]{:S(2)}) collective-permute-start(f32[8,2,8,128]{3,2,1,0:T(8,128)S(1)} %pad_maximum_fusion), channel_id=1, source_target_pairs={{0,0},{1,96},{2,192},{3,288},{4,384},{5,480},{6,576},{7,672},{8,12... | collective-permute-start | bytes 196616 | tf_op jit(solution)/shard_map/ppermute | solution.py:397
  40.9 5.2 %all-to-all-done = bf16[96,10,4,128]{3,2,1,0:T(4,128)(2,1)S(1)} async-done(((bf16[96,10,4,128]{3,2,1,0:T(4,128)(2,1)}), bf16[96,10,4,128]{3,2,1,0:T(4,128)(2,1)S(1)}, u32[]{:S(2)}, u32[]{:S(2)}) %all-to-all-start) | async-done | bytes 983072 | tf_op jit(solution)/shard_map/all_to_all | solution.py:398
  46.0 0.2 copy.34
  46.2 0.3 fusion
  46.6 0.1 copy_bitcast_fusion.1
  46.7 4.6 %collective-permute-done = f32[8,2,8,128]{3,2,1,0:T(8,128)} collective-permute-done((f32[8,2,8,128]{3,2,1,0:T(8,128)S(1)}, f32[8,2,8,128]{3,2,1,0:T(8,128)}, u32[]{:S(2)}, u32[]{:S(2)}) %collective-permute-start) | collective-permute-done | bytes 65568 | tf_op jit(solution)/shard_map/ppermute | solution.py:397
  51.3 14.7 %all-to-all-start.1 = ((f32[8,2,8,128]{3,2,1,0:T(8,128)}), f32[8,2,8,128]{3,2,1,0:T(8,128)S(1)}, u32[]{:S(2)}, u32[]{:S(2)}) async-start(f32[8,2,8,128]{3,2,1,0:T(8,128)} %collective-permute-done), calls=%async_computation.1 | async-start | bytes 131072 | tf_op jit(solution)/shard_map/all_to_all | solution.py:403
  66.0 4.9 %collective-permute-start.1 = (bf16[12,10,4,128]{3,2,1,0:T(4,128)(2,1)S(1)}, bf16[12,10,4,128]{3,2,1,0:T(4,128)(2,1)S(1)}, u32[]{:S(2)}, u32[]{:S(2)}) collective-permute-start(bf16[12,10,4,128]{3,2,1,0:T(4,128)(2,1)S(1)} %get-tuple-element.8), channel_id=1, source_target_pairs={{0,96},{12,108},{24,120},{36,132},{48,144},{60,156},{72,168},{84,1... | collective-permute-start | bytes 368648 | tf_op jit(solution)/shard_map/ppermute | solution.py:401
  70.9 4.3 %collective-permute-start.2 = (bf16[12,10,4,128]{3,2,1,0:T(4,128)(2,1)S(1)}, bf16[12,10,4,128]{3,2,1,0:T(4,128)(2,1)S(1)}, u32[]{:S(2)}, u32[]{:S(2)}) collective-permute-start(bf16[12,10,4,128]{3,2,1,0:T(4,128)(2,1)S(1)} %get-tuple-element.9), channel_id=1, source_target_pairs={{96,0},{108,12},{120,24},{132,36},{144,48},{156,60},{168,72},{180,... | collective-permute-start | bytes 368648 | tf_op jit(solution)/shard_map/ppermute | solution.py:402
  75.2 0.5 sqrt.7.ep_ref
  75.7 1.5 %copy.28.r_ref = bf16[12,8,10,4,128]{4,3,2,1,0:T(4,128)(2,1)} copy(bf16[12,8,10,4,128]{4,1,0,3,2:T(8,128)(2,1)S(1)} %bitcast.20) | data formatting | bytes 1966080 | tf_op jit(solution)/shard_map/reshape | solution.py:399
  77.2 6.5 %collective-permute-done.2.high_ref = bf16[12,10,4,128]{3,2,1,0:T(4,128)(2,1)S(1)} collective-permute-done((bf16[12,10,4,128]{3,2,1,0:T(4,128)(2,1)S(1)}, bf16[12,10,4,128]{3,2,1,0:T(4,128)(2,1)S(1)}, u32[]{:S(2)}, u32[]{:S(2)}) %collective-permute-start.2) | collective-permute-done | bytes 122912 | tf_op jit(solution)/shard_map/ppermute | solution.py:402
  83.7 0.7 copy-done.2
  84.3 0.6 copy-done
  85.0 15.1 %analysis.1 = bf16[12,8,8,4,128]{4,3,2,1,0:T(4,128)(2,1)} custom-call(f32[4]{0:T(128)} %sqrt.7.ep_ref, bf16[12,8,10,4,128]{4,3,2,1,0:T(4,128)(2,1)} %copy.28.r_ref, bf16[12,10,4,128]{3,2,1,0:T(4,128)(2,1)} %copy-done.1, bf16[12,10,4,128]{3,2,1,0:T(4,128)(2,1)} %copy-done.2, f32[8,2,8,128]{3,2,1,0:T(8,128)} %copy-done), custom_call_target="tpu_custom_call" | custom-call | tf_op jit(solution)/shard_map/analysis/pallas_call | solution.py:405
  100.1 40.8 %all_to_all.15.o_ref = bf16[96,8,4,128]{3,2,1,0:T(4,128)(2,1)} all-to-all(bf16[96,8,4,128]{3,2,1,0:T(4,128)(2,1)} %bitcast.21), channel_id=1, replica_groups={{0,12,24,36,48,60,72,84,1,13,25,37,49,61,73,85,2,14,26,38,50,62,74,86,3..., dimensions={0} | all-to-all | bytes 1572864 | tf_op jit(solution)/shard_map/all_to_all | solution.py:424
  140.9 2.9 %unpack.1 = bf16[4,2,4,12288]{3,2,1,0:T(4,128)(2,1)} custom-call(bf16[96,8,4,128]{3,2,1,0:T(4,128)(2,1)} %all_to_all.15.o_ref), custom_call_target="tpu_custom_call" | custom-call | tf_op jit(solution)/shard_map/unpack/pallas_call | solution.py:428
  (24 shorter events, 0.5 us)
Async XLA Ops:
  8.8 12.9 %copy-start.3 = (f32[128,4,16]{0,2,1:T(8,128)S(1)}, f32[128,4,16]{0,2,1:T(8,128)}, u32[]{:S(2)}) copy-start(f32[128,4,16]{0,2,1:T(8,128)} %param.15) | copy-start | bytes 98308
  8.8 37.3 %all-to-all-start = ((bf16[96,10,4,128]{3,2,1,0:T(4,128)(2,1)}), bf16[96,10,4,128]{3,2,1,0:T(4,128)(2,1)S(1)}, u32[]{:S(2)}, u32[]{:S(2)}) async-start(bf16[96,10,4,128]{3,2,1,0:T(4,128)(2,1)} %pack.1), calls=%async_computation | async-start | bytes 1966080 | tf_op jit(solution)/shard_map/all_to_all | solution.py:398
  21.9 0.8 copy-start.4
  22.0 0.7 copy-start.6
  22.8 0.7 copy-start.5
  23.8 27.5 %collective-permute-start = (f32[8,2,8,128]{3,2,1,0:T(8,128)S(1)}, f32[8,2,8,128]{3,2,1,0:T(8,128)}, u32[]{:S(2)}, u32[]{:S(2)}) collective-permute-start(f32[8,2,8,128]{3,2,1,0:T(8,128)S(1)} %pad_maximum_fusion), channel_id=1, source_target_pairs={{0,0},{1,96},{2,192},{3,288},{4,384},{5,480},{6,576},{7,672},{8,12... | collective-permute-start | bytes 196616 | tf_op jit(solution)/shard_map/ppermute | solution.py:397
  51.3 23.9 %copy-start.7 = (f32[4]{0:T(128)S(1)}, f32[4]{0:T(128)}, u32[]{:S(2)}) copy-start(f32[4]{0:T(128)} %param.16) | copy-start | bytes 52
  51.3 32.4 %all-to-all-start.1 = ((f32[8,2,8,128]{3,2,1,0:T(8,128)}), f32[8,2,8,128]{3,2,1,0:T(8,128)S(1)}, u32[]{:S(2)}, u32[]{:S(2)}) async-start(f32[8,2,8,128]{3,2,1,0:T(8,128)} %collective-permute-done), calls=%async_computation.1 | async-start | bytes 131072 | tf_op jit(solution)/shard_map/all_to_all | solution.py:403
  66.0 11.2 %collective-permute-start.1 = (bf16[12,10,4,128]{3,2,1,0:T(4,128)(2,1)S(1)}, bf16[12,10,4,128]{3,2,1,0:T(4,128)(2,1)S(1)}, u32[]{:S(2)}, u32[]{:S(2)}) collective-permute-start(bf16[12,10,4,128]{3,2,1,0:T(4,128)(2,1)S(1)} %get-tuple-element.8), channel_id=1, source_target_pairs={{0,96},{12,108},{24,120},{36,132},{48,144},{60,156},{72,168},{84,1... | collective-permute-start | bytes 368648 | tf_op jit(solution)/shard_map/ppermute | solution.py:401
  70.9 12.8 %collective-permute-start.2 = (bf16[12,10,4,128]{3,2,1,0:T(4,128)(2,1)S(1)}, bf16[12,10,4,128]{3,2,1,0:T(4,128)(2,1)S(1)}, u32[]{:S(2)}, u32[]{:S(2)}) collective-permute-start(bf16[12,10,4,128]{3,2,1,0:T(4,128)(2,1)S(1)} %get-tuple-element.9), channel_id=1, source_target_pairs={{96,0},{108,12},{120,24},{132,36},{144,48},{156,60},{168,72},{180,... | collective-permute-start | bytes 368648 | tf_op jit(solution)/shard_map/ppermute | solution.py:402
  77.2 6.5 %copy-start.1 = (bf16[12,10,4,128]{3,2,1,0:T(4,128)(2,1)}, bf16[12,10,4,128]{3,2,1,0:T(4,128)(2,1)S(1)}, u32[]{:S(2)}) copy-start(bf16[12,10,4,128]{3,2,1,0:T(4,128)(2,1)S(1)} %collective-permute-done.1.low_ref) | copy-start | bytes 368644
  83.7 0.7 copy-start.2
  84.3 0.6 copy-start
